TPU v7x, 768 devices: a whole 4x8x12 slice. The times are simulated.
768 devices in a mesh: feat: 12 (over z), dom: 64 (over y, x, core).
Axes of the slice: x: 4, y: 8, z: 12, core: 2. Of those that a mesh axis runs over, the one named last changes fastest.
Arguments:
- features: bfloat16 [64, 1536, 768], P('dom', None, 'feat'), may hold values from -6 to 6
- tiles: bfloat16 [64, 36, 128, 128], P('dom')
- tile_ids: int32 [64, 36, 2], P('dom'), may hold values from 0 to 11, as said below
- sources: int32 [64, 64, 12, 16], P('dom'), may hold values from 0 to 1535
- targets: int32 [64, 64, 12, 16], P('dom'), may hold values from 0 to 127
- counts: int32 [64, 64, 12], P('dom'), may hold values from 0 to 16, as said below
- edge_weight: bfloat16 [64, 64, 12, 16], P('dom'), may hold values from 0.5 to 2
- self_one: bfloat16 [768, 1024], replicated, may hold values from -0.21875 to 0.21875
- neigh_one: bfloat16 [768, 1024], replicated, may hold values from -0.21875 to 0.21875
- self_out: bfloat16 [1024, 153], replicated, may hold values from -0.1875 to 0.1875
- neigh_out: bfloat16 [1024, 153], replicated, may hold values from -0.1875 to 0.1875
Outputs:
- hidden: bfloat16 [64, 1536, 1024], P('dom', 'feat')
- logits: float32 [64, 153, 1536], P('dom', None, 'feat')
Inputs may be any that keep to these rules, and one draw needn't show every extreme that they name: `tile_ids`: in each partition the 36 (row block, column block) pairs are distinct, and every row block appears in exactly 3 of them, in no fixed order. counts[e, e, g] is 0; in every draw some partition receives 16 live slots from every other partition in every group.
All inputs are finite; a program needn't handle non-finite values.
Results may differ from a plain program's by a relative error of at most 0.003.
Values may be sent and summed in bfloat16 or wider, within the bound.
A program may use at most 64 MiB of HBM per device.

v0:
```python
import jax
import jax.numpy as jnp
from jax import lax
from jax.sharding import PartitionSpec as P

precise = lax.Precision.HIGHEST


def on_device(
    features,
    tiles,
    tile_ids,
    sources,
    targets,
    counts,
    edge_weight,
    self_one,
    neigh_one,
    self_out,
    neigh_out,
):
    feature_cols = features[0]
    tile_contents = tiles[0]
    tile_pairs = tile_ids[0]
    groups = lax.axis_size("feat")
    group_index = lax.axis_index("feat")
    part_nodes = feature_cols.shape[0]
    row_count = part_nodes // groups
    tile_side = tile_contents.shape[1]
    block_count = part_nodes // tile_side
    slots = sources.shape[3]
    owners = (
        tile_pairs[:, 0][:, None] == jnp.arange(block_count, dtype=jnp.int32)[None, :]
    ).astype(jnp.float32)
    slot_live = jnp.arange(slots, dtype=jnp.int32)[None, None, :] < counts[0][:, :, None]
    kept_weights = jnp.where(slot_live, edge_weight[0], jnp.zeros((), jnp.bfloat16))
    target_hits = targets[0][..., None] == jnp.arange(row_count, dtype=jnp.int32)
    edge_matrices = jnp.where(target_hits, kept_weights[..., None], jnp.zeros((), jnp.bfloat16))
    tile_rows = jnp.sum(tile_contents, axis=2, dtype=jnp.float32)
    local_degree = jnp.einsum("tb,ti->bi", owners, tile_rows, precision=precise).reshape(part_nodes)
    edge_degree = jnp.sum(edge_matrices, axis=(0, 2), dtype=jnp.float32).reshape(part_nodes)
    degree = local_degree + edge_degree
    col_blocks = feature_cols.reshape(block_count, tile_side, feature_cols.shape[1])
    picked = jnp.take(col_blocks, tile_pairs[:, 1], axis=0)
    products = jnp.einsum("tij,tjc->tic", tile_contents, picked, preferred_element_type=jnp.float32)
    local_term = jnp.einsum("tb,tic->bic", owners, products, precision=precise).reshape(
        part_nodes, feature_cols.shape[1]
    )
    outgoing = jnp.take(feature_cols, sources[0], axis=0)
    incoming = lax.all_to_all(outgoing, "dom", split_axis=0, concat_axis=0, tiled=True)
    edge_term = jnp.einsum(
        "dgsr,dgsc->grc", edge_matrices, incoming, preferred_element_type=jnp.float32
    )
    edge_term = edge_term.reshape(part_nodes, feature_cols.shape[1])
    neighbours = ((local_term + edge_term) / degree[:, None]).astype(jnp.bfloat16)
    feature_rows, neighbour_rows = (
        lax.all_to_all(feature_cols, "feat", split_axis=0, concat_axis=1, tiled=True),
        lax.all_to_all(neighbours, "feat", split_axis=0, concat_axis=1, tiled=True),
    )
    preact = jnp.dot(feature_rows, self_one, preferred_element_type=jnp.float32)
    preact = preact + jnp.dot(neighbour_rows, neigh_one, preferred_element_type=jnp.float32)
    hidden = jnp.maximum(preact, 0.0).astype(jnp.bfloat16)
    blocks_mine = row_count // tile_side
    first_block = group_index * blocks_mine
    row_pick = (
        tile_pairs[:, 0][:, None] == first_block + jnp.arange(blocks_mine, dtype=jnp.int32)[None, :]
    )
    col_pick = tile_pairs[:, 1][:, None] == jnp.arange(block_count, dtype=jnp.int32)[None, :]
    tile_positions = (row_pick[:, :, None] & col_pick[:, None, :]).astype(jnp.bfloat16)
    tile_band_rows = jnp.einsum(
        "mwr,mqy->wqry", tile_positions, tile_contents, preferred_element_type=jnp.float32
    )
    tile_band_rows = tile_band_rows.astype(jnp.bfloat16).reshape(row_count, part_nodes)
    group_mats = lax.dynamic_index_in_dim(edge_matrices, group_index, 1, keepdims=False)
    group_degree = lax.dynamic_slice_in_dim(degree, group_index * row_count, row_count)
    send_ids = lax.dynamic_index_in_dim(sources[0], group_index, 1, keepdims=False)
    own_term = lax.dot_general(
        self_out, hidden, (((0,), (1,)), ((), ())), preferred_element_type=jnp.float32
    )
    start_pick = jnp.zeros(send_ids.shape + (hidden.shape[1],), jnp.bfloat16)
    received = lax.all_gather(hidden, "feat", axis=0, tiled=True)
    chosen = start_pick
    piece_rows = received.shape[0]
    summed = jnp.dot(tile_band_rows, received, preferred_element_type=jnp.float32)
    inside = (send_ids >= 0) & (send_ids < piece_rows)
    picked_rows = jnp.take(received, jnp.clip(send_ids, 0, piece_rows - 1), axis=0)
    chosen = jnp.where(inside[..., None], picked_rows, chosen)
    summed, chosen = (summed, chosen)
    arrived = lax.all_to_all(chosen, "dom", split_axis=0, concat_axis=0, tiled=True)
    summed = summed + jnp.einsum(
        "dsr,dsc->rc", group_mats, arrived, preferred_element_type=jnp.float32
    )
    mean_two = summed / group_degree[:, None]
    logits = own_term + lax.dot_general(
        neigh_out.astype(jnp.float32), mean_two, (((0,), (1,)), ((), ())), precision=precise
    )
    return (hidden[None], logits[None])


def solution(mesh):
    placed = (
        P("dom", None, "feat"),
        P("dom", None, None, None),
        P("dom", None, None),
        P("dom", None, None, None),
        P("dom", None, None, None),
        P("dom", None, None),
        P("dom", None, None, None),
        P(),
        P(),
        P(),
        P(),
    )
    return jax.shard_map(
        on_device,
        mesh=mesh,
        in_specs=placed,
        out_specs=(P("dom", "feat", None), P("dom", None, "feat")),
        check_vma=False,
    )
```

profile of v0, /device:TPU:1, one launch (start us, length us, event | category | flops | bytes accessed | tf_op | source)
XLA Modules:
  0.0 319.6 jit_solution(3791331285048111536)
XLA Ops:
  9.6 1.1 copy.63
  11.1 43.7 %gather_fusion.1 = bf16[12288,64]{1,0:T(8,128)(2,1)} fusion(bf16[1536,64]{1,0:T(8,128)(2,1)S(1)} %bitcast.92, s32[12288]{0:T(1024)S(1)} %broadcast_clamp_fusion), kind=kCustom, calls=%fused_computation.1 | custom fusion | bytes 3194880 | tf_op jit(solution)/shard_map/jit(_take)/gather | solution.py:49
  54.8 7.0 %broadcast_select_fusion = bf16[64,12,16,64]{3,2,1,0:T(8,128)(2,1)} fusion(bf16[64,12,16,64]{3,2,1,0:T(8,128)(2,1)} %bitcast.93, pred[64,12,16]{2,1,0:T(8,128)(4,1)S(1)} %copy.62), kind=kLoop, calls=%fused_computation.8 | loop fusion | flops 786432 | bytes 3158016 | tf_op jit(solution)/shard_map/jit(_take)/select_n | solution.py:49
  61.7 6.2 %reshape.240 = bf16[64,2,6144]{2,1,0:T(2,128)(2,1)} reshape(bf16[64,12,16,64]{3,2,1,0:T(8,128)(2,1)} %broadcast_select_fusion) | data formatting | bytes 3145728
  67.9 15.5 %all-to-all-start.1 = ((bf16[64,2,6144]{2,1,0:T(2,128)(2,1)}), bf16[64,2,6144]{2,1,0:T(2,128)(2,1)}, u32[]{:S(2)}, u32[]{:S(2)}) async-start(bf16[64,2,6144]{2,1,0:T(2,128)(2,1)} %reshape.240), calls=%async_computation.1 | async-start | bytes 3145728 | tf_op jit(solution)/shard_map/all_to_all | solution.py:50
  84.4 1.6 gather_fusion
  87.3 4.2 %convert_reduce_fusion = f32[12,128]{1,0:T(8,128)S(1)} fusion(bf16[64,12,16]{0,2,1:T(8,128)(2,1)S(1)} %fusion.40, s32[64,12,16]{0,2,1:T(8,128)S(1)} %bitcast.99), kind=kLoop, calls=%fused_computation.3 | loop fusion | flops 6289920 | bytes 79872 | tf_op jit(solution)/shard_map/reduce_sum | solution.py:41
  91.6 2.0 convolution_bitcast_fusion
  93.5 29.0 %all-to-all-done.1 = bf16[64,2,6144]{2,1,0:T(2,128)(2,1)} async-done(((bf16[64,2,6144]{2,1,0:T(2,128)(2,1)}), bf16[64,2,6144]{2,1,0:T(2,128)(2,1)}, u32[]{:S(2)}, u32[]{:S(2)}) %all-to-all-start.1) | async-done | bytes 1572896 | tf_op jit(solution)/shard_map/all_to_all | solution.py:50
  122.5 11.2 %all-to-all-start = ((bf16[12,128,64]{1,2,0:T(8,128)(2,1)}), bf16[12,128,64]{1,2,0:T(8,128)(2,1)S(1)}, u32[]{:S(2)}, u32[]{:S(2)}) async-start(bf16[12,128,64]{1,2,0:T(8,128)(2,1)} %copy.59), calls=%async_computation | async-start | bytes 393216 | tf_op jit(solution)/shard_map/all_to_all | solution.py:57
  133.7 6.4 %reshape.241 = bf16[64,12,16,64]{3,2,1,0:T(8,128)(2,1)} reshape(bf16[64,2,6144]{2,1,0:T(2,128)(2,1)} %all-to-all-done.1) | data formatting | bytes 3145728
  140.1 10.0 %fusion.30 = f32[12,128,64]{1,2,0:T(8,128)S(1)} fusion(bf16[64,12,16,64]{3,2,1,0:T(8,128)(2,1)} %reshape.241, s32[64,12,16]{0,2,1:T(8,128)S(1)} %bitcast.100, bf16[64,12,16]{0,2,1:T(8,128)(2,1)S(1)} %fusion.40), kind=kOutput, calls=%fused_computation.29 | convolution fusion | flops 204472320 | bytes 2039808 | tf_op jit(solution)/shard_map/dgsr,dgsc->grc/dot_general | solution.py:51
  150.1 1.4 fusion.26
  152.2 9.1 %all-to-all-start.2 = ((bf16[12,128,64]{1,2,0:T(8,128)(2,1)}), bf16[12,128,64]{1,2,0:T(8,128)(2,1)}, u32[]{:S(2)}, u32[]{:S(2)}) async-start(bf16[12,128,64]{1,2,0:T(8,128)(2,1)} %copy.67), calls=%async_computation.2 | async-start | bytes 393216 | tf_op jit(solution)/shard_map/all_to_all | solution.py:58
  161.7 10.7 %all-to-all-done.2 = bf16[12,128,64]{1,2,0:T(8,128)(2,1)} async-done(((bf16[12,128,64]{1,2,0:T(8,128)(2,1)}), bf16[12,128,64]{1,2,0:T(8,128)(2,1)}, u32[]{:S(2)}, u32[]{:S(2)}) %all-to-all-start.2) | async-done | bytes 196640 | tf_op jit(solution)/shard_map/all_to_all | solution.py:58
  172.4 2.6 fusion.29
  177.6 49.4 %all-gather.2.cloned.1.call-done = bf16[1536,1024]{1,0:T(8,128)(2,1)} async-done(((bf16[128,1024]{1,0:T(8,128)(2,1)}), bf16[1536,1024]{1,0:T(8,128)(2,1)}) %all-gather.2.cloned.1.call-update) | async-done | bytes 3145744 | tf_op jit(solution)/shard_map/all_gather | solution.py:81
  227.0 8.3 %gather_fusion.2 = bf16[1024,1024]{1,0:T(8,128)(2,1)} fusion(bf16[1536,1024]{1,0:T(8,128)(2,1)} %all-gather.2.cloned.1.call-done, s32[1024]{0:T(1024)S(1)} %broadcast_clamp_fusion.1), kind=kCustom, calls=%fused_computation.2 | custom fusion | bytes 4198400 | tf_op jit(solution)/shard_map/jit(_take)/gather | solution.py:86
  235.3 2.8 select_select_fusion
  238.1 17.1 %all-to-all-start.3 = ((bf16[64,16,1024]{2,1,0:T(8,128)(2,1)}), bf16[64,16,1024]{2,1,0:T(8,128)(2,1)}, u32[]{:S(2)}, u32[]{:S(2)}) async-start(bf16[64,16,1024]{2,1,0:T(8,128)(2,1)} %select_select_fusion), calls=%async_computation.3 | async-start | bytes 4194304 | tf_op jit(solution)/shard_map/all_to_all | solution.py:89
  257.4 6.6 %fusion = bf16[64,12,16,128]{3,0,2,1:T(8,128)(2,1)} fusion(s32[64,12,16]{0,2,1:T(8,128)S(1)} %bitcast.101, bf16[64,12,16]{0,2,1:T(8,128)(2,1)S(1)} %fusion.40), kind=kLoop, calls=%fused_computation.5 | loop fusion | flops 3145728 | bytes 3219456 | tf_op jit(solution)/shard_map/jit(_where)/select_n | solution.py:38
  264.2 40.6 %all-to-all-done.3 = bf16[64,16,1024]{2,1,0:T(8,128)(2,1)} async-done(((bf16[64,16,1024]{2,1,0:T(8,128)(2,1)}), bf16[64,16,1024]{2,1,0:T(8,128)(2,1)}, u32[]{:S(2)}, u32[]{:S(2)}) %all-to-all-start.3) | async-done | bytes 2097184 | tf_op jit(solution)/shard_map/all_to_all | solution.py:89
  304.8 4.1 %fusion.16 = f32[128,1024]{1,0:T(8,128)S(1)} fusion(bf16[64,16,1024]{2,1,0:T(8,128)(2,1)} %all-to-all-done.3, bf16[64,12,16,128]{3,0,2,1:T(8,128)(2,1)} %fusion, s32[]{:T(128)S(6)} %select_n.83), kind=kOutput, calls=%fused_computation.22 | convolution fusion | flops 268435456 | bytes 2883588 | tf_op jit(solution)/shard_map/dsr,dsc->rc/dot_general | solution.py:90
  309.0 2.5 fusion.12
  (60 shorter events, 12.2 us)
Async XLA Ops:
  7.2 154.1 %copy-start = (bf16[768,1024]{1,0:T(8,128)(2,1)S(1)}, bf16[768,1024]{1,0:T(8,128)(2,1)}, u32[]{:S(2)}) copy-start(bf16[768,1024]{1,0:T(8,128)(2,1)} %param.18) | copy-start | bytes 4718596
  67.9 15.6 %copy-start.5 = (bf16[1,1536,64]{1,2,0:T(8,128)(2,1)S(1)}, bf16[1,1536,64]{1,2,0:T(8,128)(2,1)}, u32[]{:S(2)}) copy-start(bf16[1,1536,64]{1,2,0:T(8,128)(2,1)} %param.11) | copy-start | bytes 589828
  67.9 16.5 %copy-start.11 = (s32[1,64,12]{1,0,2:T(1,128)S(1)}, s32[1,64,12]{1,0,2:T(1,128)}, u32[]{:S(2)}) copy-start(s32[1,64,12]{1,0,2:T(1,128)} %param.16) | copy-start | bytes 9220
  67.9 16.5 %copy-start.12 = (s32[1,36,2]{1,2,0:T(2,128)S(1)}, s32[1,36,2]{1,2,0:T(2,128)}, u32[]{:S(2)}) copy-start(s32[1,36,2]{1,2,0:T(2,128)} %param.13) | copy-start | bytes 868
  67.9 54.6 %all-to-all-start.1 = ((bf16[64,2,6144]{2,1,0:T(2,128)(2,1)}), bf16[64,2,6144]{2,1,0:T(2,128)(2,1)}, u32[]{:S(2)}, u32[]{:S(2)}) async-start(bf16[64,2,6144]{2,1,0:T(2,128)(2,1)} %reshape.240), calls=%async_computation.1 | async-start | bytes 3145728 | tf_op jit(solution)/shard_map/all_to_all | solution.py:50
  83.5 2.6 copy-start.1
  83.6 3.6 %copy-start.6 = (s32[1,64,12,16]{1,3,2,0:T(8,128)S(1)}, s32[1,64,12,16]{1,3,2,0:T(8,128)}, u32[]{:S(2)}) copy-start(s32[1,64,12,16]{1,3,2,0:T(8,128)} %param.15) | copy-start | bytes 147460
  122.5 29.6 %all-to-all-start = ((bf16[12,128,64]{1,2,0:T(8,128)(2,1)}), bf16[12,128,64]{1,2,0:T(8,128)(2,1)S(1)}, u32[]{:S(2)}, u32[]{:S(2)}) async-start(bf16[12,128,64]{1,2,0:T(8,128)(2,1)} %copy.59), calls=%async_computation | async-start | bytes 393216 | tf_op jit(solution)/shard_map/all_to_all | solution.py:57
  133.7 6.4 %copy-start.7 = (s32[1,64,12,16]{1,3,2,0:T(8,128)S(1)}, s32[1,64,12,16]{1,3,2,0:T(8,128)}, u32[]{:S(2)}) copy-start(s32[1,64,12,16]{1,3,2,0:T(8,128)} %param.15) | copy-start | bytes 147460
  140.1 10.0 %copy-start.4 = (f32[36,128,64]{1,2,0:T(8,128)S(1)}, f32[36,128,64]{1,2,0:T(8,128)}, u32[]{:S(2)}) copy-start(f32[36,128,64]{1,2,0:T(8,128)} %convolution_bitcast_fusion) | copy-start | bytes 3538948
  152.2 20.2 %all-to-all-start.2 = ((bf16[12,128,64]{1,2,0:T(8,128)(2,1)}), bf16[12,128,64]{1,2,0:T(8,128)(2,1)}, u32[]{:S(2)}, u32[]{:S(2)}) async-start(bf16[12,128,64]{1,2,0:T(8,128)(2,1)} %copy.67), calls=%async_computation.2 | async-start | bytes 393216 | tf_op jit(solution)/shard_map/all_to_all | solution.py:58
  161.2 65.8 %all-gather.2.cloned.1.call-start = ((), (), s32[]{:S(2)}) async-start(), calls=%async_computation.4 | async-start | bytes 3407872 | tf_op jit(solution)/shard_map/all_gather | solution.py:81
  238.1 66.7 %all-to-all-start.3 = ((bf16[64,16,1024]{2,1,0:T(8,128)(2,1)}), bf16[64,16,1024]{2,1,0:T(8,128)(2,1)}, u32[]{:S(2)}, u32[]{:S(2)}) async-start(bf16[64,16,1024]{2,1,0:T(8,128)(2,1)} %select_select_fusion), calls=%async_computation.3 | async-start | bytes 4194304 | tf_op jit(solution)/shard_map/all_to_all | solution.py:89
  255.2 2.1 copy-start.8
  256.1 7.8 %copy-start.2 = (bf16[128,1024]{1,0:T(8,128)(2,1)S(1)}, bf16[128,1024]{1,0:T(8,128)(2,1)}, u32[]{:S(2)}) copy-start(bf16[128,1024]{1,0:T(8,128)(2,1)} %fusion.29) | copy-start | bytes 786436
  256.2 7.8 %copy-start.9 = (bf16[1024,153]{0,1:T(8,128)(2,1)S(1)}, bf16[1024,153]{0,1:T(8,128)(2,1)}, u32[]{:S(2)}) copy-start(bf16[1024,153]{0,1:T(8,128)(2,1)} %param.20) | copy-start | bytes 940036
  264.0 45.0 %copy-start.3 = (bf16[1,128,12,128]{1,3,2,0:T(8,128)(2,1)S(1)}, bf16[1,128,12,128]{1,3,2,0:T(8,128)(2,1)}, u32[]{:S(2)}) copy-start(bf16[1,128,12,128]{1,3,2,0:T(8,128)(2,1)} %copy.69) | copy-start | bytes 1179652
  309.0 2.6 copy-start.10
Sparse Core Ops, SparseCore 0:
  175.2 51.7 all-gather.1
where the time goes:
time: 322 us; the launch traced here: 320 us
  waiting for transfers between devices  130 us (40%)
  local copies, waits for them, and re-layouts  72 us (22%)
  starting transfers between devices  52.9 us (16%)
  other arithmetic  25.9 us (8%)
  matrix products  24.7 us (8%)
  between operations  14.3 us (4%)
    all_gather x1, waiting for transfers between devices, on_device(): received = lax.all_gather(hidden, 'feat', axis=0, tiled=True)  49.4 us
    gather x1, local copies, waits for them, and re-layouts, on_device(): outgoing = jnp.take(feature_cols, sources[0], axis=0)  43.7 us
    all_to_all x1, waiting for transfers between devices, on_device(): lax.all_to_all(chosen, 'dom', split_axis=0, concat_axis=0, tiled=True)  40.6 us
    all_to_all x1, waiting for transfers between devices, on_device(): lax.all_to_all(outgoing, 'dom', split_axis=0, concat_axis=0, tiled=True)  29 us
    all_to_all x1, starting transfers between devices, on_device(): lax.all_to_all(chosen, 'dom', split_axis=0, concat_axis=0, tiled=True)  17.1 us
    all_to_all x1, starting transfers between devices, on_device(): lax.all_to_all(outgoing, 'dom', split_axis=0, concat_axis=0, tiled=True)  15.5 us
    unnamed x31, local copies, waits for them, and re-layouts  14.5 us
    all_to_all x1, starting transfers between devices, on_device(): lax.all_to_all(feature_cols, 'feat', split_axis=0, concat_axis=1, tiled=T...  11.2 us
  transfers between devices with their start and end apart: 5, of which 4 were waited for; matrix products, arithmetic and copies ran while one was open for 13% of the time, Pallas kernels for 0%

commit v1 on v0

v1 whole, which is shorter than its diff:
```python
import jax
import jax.numpy as jnp
from jax import lax
from jax.experimental import pallas as pl
from jax.experimental.pallas import tpu as pltpu
from jax.sharding import PartitionSpec as P

MESH = pl.DeviceIdType.MESH
BF = jnp.bfloat16
F32 = jnp.float32
I32 = jnp.int32
NT = (((1,), (1,)), ((), ()))

NF = 12
ND = 64
NY = 8
NX = 8
COLS = 64
NODES = 1536
HID = 1024
CLS = 153
CPAD = 160
PAIRS = ((0, 1), (2, 7), (6, 3), (4, 5))


def iota(shape, dim):
    return lax.broadcasted_iota(I32, shape, dim)


def mod(a, n):
    return lax.rem(a, jnp.int32(n))


def dot(a, b):
    return jnp.dot(a, b, preferred_element_type=F32)


def dot_nt(a, b):
    return lax.dot_general(a, b, NT, preferred_element_type=F32)


def kernel(
    ids, counts, sources, targets, weights, feat, tiles_hbm, s1_hbm, n1_hbm, so, no,
    hidden_ref, logits_ref,
    tiles, s1, n1, tab, idx_out, idx_in, picked, out1, in1, ftd, scat, rows_t, rows_w, acc,
    frows, nsend_buf, nrows, pre, wso, wno, z, oh2, scat2, out2, in2, deg, prod, band,
    loc, tsend, trecv, isend, irecv, fsend, frecv, xsend, xrecv, nsend, nrecv, zsend, zrecv, asend, arecv,
):
    f = lax.axis_index("feat")
    d = lax.axis_index("dom")
    y = lax.div(d, jnp.int32(NX))
    xc = mod(d, NX)
    core = mod(d, 2)

    loads = [
        pltpu.make_async_copy(tiles_hbm, tiles, loc.at[0]),
        pltpu.make_async_copy(s1_hbm, s1, loc.at[1]),
        pltpu.make_async_copy(n1_hbm, n1, loc.at[2]),
    ]
    for load in loads:
        load.start()

    def remote(src, dst, ss, rs, fi, di):
        return pltpu.make_async_remote_copy(
            src_ref=src, dst_ref=dst, send_sem=ss, recv_sem=rs, device_id=(fi, di), device_id_type=MESH
        )

    def arrived(dst, rs):
        pltpu.make_async_copy(dst, dst, rs).wait()

    def row_peer(k):
        return mod(y + k, NY) * NX + xc

    def col_peer(k):
        return y * NX + mod(xc + k, NX)

    barrier = pltpu.get_barrier_semaphore()
    for k in range(1, NY):
        pl.semaphore_signal(barrier, inc=1, device_id=(f, row_peer(k)), device_id_type=MESH)
    for k in range(1, NX):
        pl.semaphore_signal(barrier, inc=1, device_id=(f, col_peer(k)), device_id_type=MESH)
    for k in range(1, NF):
        pl.semaphore_signal(barrier, inc=1, device_id=(mod(f + k, NF), d), device_id_type=MESH)

    src = sources[...].reshape(192, ND)
    both = jnp.concatenate([src >> 8, src & 255], axis=0).astype(F32).astype(BF)
    r32 = iota((32, ND), 0)
    e32 = iota((32, ND), 1)
    flip = (lax.div(r32, 4) + y) & 1
    halves = []
    for h in range(2):
        pick = (e32 == r32 * 2 + (flip ^ h)).astype(F32).astype(BF)
        got = dot_nt(pick, both)
        halves.append((got[:, :192] * 256.0 + got[:, 192:]).astype(I32))
    for q in range(3):
        tile = jnp.concatenate([halves[0][:, q * 64 : q * 64 + 64], halves[1][:, q * 64 : q * 64 + 64]], axis=1)
        for row in range(NY):
            idx_out[row, q * 4 : q * 4 + 4, :] = tile[row * 4 : row * 4 + 4]
    idx_in[0] = idx_out[y]

    pl.semaphore_wait(barrier, NY - 1 + NX - 1 + NF - 1)

    sent = []

    def go(copy):
        copy.start()
        sent.append(copy)

    def table(slot):
        return feat if slot == 0 else tab.at[slot]

    def pass_on(from_slot, to_slot, half, di):
        part = pl.ds(half * 768, 768)
        go(remote(
            table(from_slot).at[:, part], tab.at[to_slot, :, part],
            tsend.at[to_slot, half], trecv.at[to_slot, half], f, di,
        ))

    def took(slot, half):
        arrived(tab.at[slot, :, pl.ds(half * 768, 768)], trecv.at[slot, half])

    up = row_peer(1)
    down = row_peer(NY - 1)
    for half in range(2):
        pass_on(0, 1, half, up)
        pass_on(0, 7, half, down)
    for k in range(1, NY):
        to = mod(y + k, NY)
        go(remote(idx_out.at[to], idx_in.at[k], isend.at[k], irecv.at[k], f, to * NX + xc))
    for k in range(1, NF):
        g = mod(f + k, NF)
        go(remote(
            feat.at[:, pl.ds(pl.multiple_of(g * 128, 128), 128)], frows.at[f], fsend.at[k], frecv.at[k], g, d
        ))
    frows[f] = feat[:, pl.ds(pl.multiple_of(f * 128, 128), 128)]

    def gather(slot):
        @pl.loop(0, 6)
        def _(r):
            here = table(slot)
            wide = jnp.concatenate([here[:, k * 256 : k * 256 + 256] for k in range(6)], axis=0)
            pick = jnp.concatenate(
                [idx_in[slot, pl.ds(2 * r, 1), :], idx_in[slot, pl.ds(2 * r + 1, 1), :]], axis=1
            )
            low = pick & 255
            high = pick >> 8
            one_hot = (iota((256, 256), 0) == low).astype(F32).astype(BF)
            got = dot(wide, one_hot)
            kept = jnp.zeros((COLS, 256), F32)
            for k in range(6):
                kept = jnp.where(high == k, got[k * COLS : k * COLS + COLS], kept)
            picked[slot, :, pl.ds(pl.multiple_of(r * 256, 256), 256)] = kept.astype(BF)

    first_half = iota((COLS, 128), 1) < 64

    def merge_and_send(b):
        even, odd = PAIRS[b]
        for q in range(3):
            for col in range(4):
                at = (q * 4 + col) * 128
                one = picked[even, :, at : at + 128]
                two = picked[odd, :, at : at + 128]
                out1[b, 2 * col, :, q * 128 : q * 128 + 128] = jnp.where(first_half, one, two)
                out1[b, 2 * col + 1, :, q * 128 : q * 128 + 128] = jnp.where(first_half, two, one)
        for k in (4, 3, 5, 2, 6, 1, 7):
            to = mod(xc + k, NX)
            go(remote(
                out1.at[b, to], in1.at[b, xc, pl.ds(0, COLS)], xsend.at[b, k], xrecv.at[b, k], f, y * NX + to
            ))
        in1[b, xc, 0:COLS] = out1[b, xc]

    gather(0)

    live = iota((NF, 16, ND), 1) < counts[...]
    t_all = jnp.where(live, targets[...], -512).reshape(192, ND)
    w_all = weights[...].reshape(192, ND)
    both = jnp.concatenate([t_all.astype(F32).astype(BF), w_all], axis=0)
    batch = lax.div(r32, 8)
    halves = []
    for h in range(2):
        par = core ^ h
        far = jnp.zeros((32, ND), I32)
        for b in range(4):
            dist = jnp.where(par == 0, PAIRS[b][0], PAIRS[b][1])
            far = jnp.where(batch == b, dist, far)
        origin = ((y + 8 - far) & 7) * 8 + (r32 & 7)
        halves.append(dot_nt((e32 == origin).astype(F32).astype(BF), both))
    for q in range(3):
        lanes = iota((32, 128), 1)
        base = (lax.div(lanes, 16) & 3) * 128
        t_tile = jnp.concatenate([halves[0][:, q * 64 : q * 64 + 64], halves[1][:, q * 64 : q * 64 + 64]], axis=1)
        w_tile = jnp.concatenate(
            [halves[0][:, 192 + q * 64 : 256 + q * 64], halves[1][:, 192 + q * 64 : 256 + q * 64]], axis=1
        )
        rows_t[q] = t_tile.astype(I32) + base
        rows_w[q] = w_tile

    def build(b):
        @pl.loop(0, 8)
        def _(i):
            r = b * 8 + i
            for q in range(3):
                t = rows_t[q, pl.ds(r, 1), :]
                w = rows_w[q, pl.ds(r, 1), :]
                scat[q, :, pl.ds(pl.multiple_of(r * 128, 128), 128)] = jnp.where(
                    iota((512, 128), 0) == t, w, 0.0
                ).astype(BF)

    def scatter(b):
        for k in range(1, NX):
            arrived(in1.at[b, mod(xc + NX - k, NX), pl.ds(0, COLS)], xrecv.at[b, k])
        for q in range(3):
            rows = jnp.concatenate([in1[b, i, :, q * 128 : q * 128 + 128] for i in range(NX)], axis=1)
            acc[:, q * 512 : q * 512 + 512] += dot_nt(rows, scat[q, :, b * 1024 : b * 1024 + 1024])

    build(0)
    in1[:, :, COLS:80, :] = jnp.ones((4, NX, 16, 384), BF)
    ftd[0:COLS] = feat[...]
    ftd[COLS:80] = jnp.ones((16, NODES), BF)

    for half in range(2):
        took(1, half)
        pass_on(1, 2, half, up)
        took(7, half)
        pass_on(7, 6, half, down)
    arrived(idx_in.at[1], irecv.at[1])
    gather(1)
    merge_and_send(0)
    arrived(idx_in.at[7], irecv.at[7])
    gather(7)
    loads[0].wait()

    @pl.loop(0, 36)
    def _(t):
        cols = jnp.zeros((80, 128), BF)
        for q in range(NF):
            cols = jnp.where(ids[1, t] == q, ftd[:, q * 128 : q * 128 + 128], cols)
        prod[t] = dot_nt(cols, tiles[t])

    @pl.loop(0, NF)
    def _(r):
        total = jnp.zeros((80, 128), F32)
        for t in range(36):
            total = total + jnp.where(ids[0, t] == r, prod[t], 0.0)
        acc[:, pl.ds(pl.multiple_of(r * 128, 128), 128)] = total

    for half in range(2):
        took(2, half)
        pass_on(2, 3, half, up)
        took(6, half)
        pass_on(6, 5, half, down)
    arrived(idx_in.at[2], irecv.at[2])
    gather(2)
    merge_and_send(1)
    arrived(idx_in.at[6], irecv.at[6])
    gather(6)
    build(1)
    build(2)
    build(3)
    scatter(0)

    took(3, 0)
    pass_on(3, 4, 0, up)
    took(5, 0)
    took(3, 1)
    took(5, 1)
    pass_on(5, 4, 1, down)
    arrived(idx_in.at[3], irecv.at[3])
    gather(3)
    merge_and_send(2)
    arrived(idx_in.at[5], irecv.at[5])
    gather(5)

    loads[1].wait()
    for k in range(1, NF):
        arrived(frows.at[mod(f + NF - k, NF)], frecv.at[k])
    pre[...] = dot(frows[...].reshape(768, 128).T, s1[...])

    wso[CLS - 9 : CPAD] = jnp.zeros((16, HID), BF)
    wno[CLS - 9 : CPAD] = jnp.zeros((16, HID), BF)
    wso[0:CLS] = so[...]
    wno[0:CLS] = no[...]

    lane = iota((ND, 1024), 1)
    spread = (lax.div(lane, 16) == iota((ND, 1024), 0)).astype(F32).astype(BF)
    t2 = jnp.where(iota((16, ND), 0) < counts[f], targets[f], -512).astype(F32).astype(BF)
    own = iota((16, 1024), 0) == (iota((16, 1024), 1) & 15)
    t_row = jnp.sum(jnp.where(own, dot(t2, spread), 0.0), axis=0, keepdims=True).astype(I32)
    w_row = jnp.sum(jnp.where(own, dot(weights[f], spread), 0.0), axis=0, keepdims=True)
    scat2[...] = jnp.where(iota((128, 1024), 0) == t_row, w_row, 0.0).astype(BF)
    s2 = sources[f]
    high2 = (s2 >> 8).astype(F32).astype(BF)
    low2 = (s2 & 255).astype(F32).astype(BF)

    @pl.loop(0, 8)
    def _(j):
        rows = iota((128, ND), 0) + j * 128
        expand = (lax.div(rows, 16) == iota((128, ND), 1)).astype(F32).astype(BF)
        value = dot_nt(expand, high2) * 256.0 + dot_nt(expand, low2)
        mine = (iota((128, 16), 0) & 15) == iota((128, 16), 1)
        node = jnp.sum(jnp.where(mine, value, 0.0), axis=1, keepdims=True).astype(I32)
        for q in range(NF):
            oh2[pl.ds(pl.multiple_of(j * 128, 128), 128), q * 128 : q * 128 + 128] = (
                (iota((128, 128), 1) + q * 128) == node
            ).astype(F32).astype(BF)

    @pl.loop(0, NF)
    def _(q):
        block = jnp.zeros((128, 128), BF)
        for t in range(36):
            block = jnp.where((ids[0, t] == f) & (ids[1, t] == q), tiles[t], block)
        band[:, pl.ds(pl.multiple_of(q * 128, 128), 128)] = block

    z[...] = jnp.zeros((256, NODES), BF)
    scatter(1)

    took(4, 0)
    took(4, 1)
    arrived(idx_in.at[4], irecv.at[4])
    gather(4)
    merge_and_send(3)
    scatter(2)
    loads[2].wait()
    scatter(3)

    for k in range(NF):
        g = mod(f + k, NF)
        part = acc[:, pl.ds(pl.multiple_of(g * 128, 128), 128)]
        mean = (part[0:COLS] / part[COLS : COLS + 1]).astype(BF)
        if k == 0:
            nrows[f] = mean
            deg[...] = part[COLS : COLS + 8]
        else:
            nsend_buf[g] = mean
            go(remote(nsend_buf.at[g], nrows.at[f], nsend.at[k], nrecv.at[k], g, d))
    for k in range(1, NF):
        arrived(nrows.at[mod(f + NF - k, NF)], nrecv.at[k])

    hidden = jnp.maximum(pre[...] + dot(nrows[...].reshape(768, 128).T, n1[...]), 0.0).astype(BF)
    hidden_ref[...] = hidden

    def block_at(g):
        return z.at[pl.ds(0, CPAD), pl.ds(pl.multiple_of(g * 128, 128), 128)]

    z[0:CPAD, pl.ds(pl.multiple_of(f * 128, 128), 128)] = dot_nt(wno[...], hidden_ref[...]).astype(BF)

    right = mod(f + 1, NF)
    left = mod(f + NF - 1, NF)

    def ring(side, k):
        g = mod(f + NF - k, NF) if side == 0 else mod(f + k, NF)
        go(remote(
            block_at(g), block_at(g), zsend.at[side, k], zrecv.at[side, k], right if side == 0 else left, d
        ))

    ring(0, 0)
    ring(1, 0)
    own_term = dot_nt(wso[...], hidden_ref[...])
    for k in range(6):
        arrived(block_at(mod(f + NF - 1 - k, NF)), zrecv.at[0, k])
        if k < 5:
            ring(0, k + 1)
            arrived(block_at(mod(f + 1 + k, NF)), zrecv.at[1, k])
        if k < 4:
            ring(1, k + 1)

    for j in range(4):
        out2[j * 256 : j * 256 + 256] = dot_nt(oh2[j * 256 : j * 256 + 256], z[...]).astype(BF)

    @pl.loop(1, ND)
    def _(k):
        to = mod(d + k, ND)
        remote(
            out2.at[pl.ds(pl.multiple_of(to * 16, 16), 16)], in2.at[pl.ds(pl.multiple_of(d * 16, 16), 16)],
            asend, arecv, f, to,
        ).start()

    mine = pl.ds(pl.multiple_of(d * 16, 16), 16)
    in2[mine] = out2[mine]
    total = dot_nt(band[...], z[...])
    arrived(in2.at[pl.ds(0, 1008)], arecv)
    total = total + dot(scat2[...], in2[...])
    logits_ref[...] = own_term[0:CLS] + (total.T)[0:CLS] / deg[0:1]

    arrived(out2.at[pl.ds(0, 1008)], asend)
    for copy in sent:
        copy.wait_send()


def on_device(
    features, tiles, tile_ids, sources, targets, counts, edge_weight, self_one, neigh_one, self_out, neigh_out
):
    vmem = pl.BlockSpec(memory_space=pltpu.VMEM)
    anywhere = pl.BlockSpec(memory_space=pl.ANY)
    dma = pltpu.SemaphoreType.DMA
    hidden, logits = pl.pallas_call(
        kernel,
        out_shape=(jax.ShapeDtypeStruct((128, HID), BF), jax.ShapeDtypeStruct((CLS, 128), F32)),
        in_specs=[pl.BlockSpec(memory_space=pltpu.SMEM)] + [vmem] * 5 + [anywhere] * 3 + [vmem] * 2,
        out_specs=(vmem, vmem),
        scratch_shapes=[
            pltpu.VMEM((36, 128, 128), BF),
            pltpu.VMEM((768, HID), BF),
            pltpu.VMEM((768, HID), BF),
            pltpu.VMEM((NY, COLS, NODES), BF),
            pltpu.VMEM((NY, 16, 128), I32),
            pltpu.VMEM((NY, 16, 128), I32),
            pltpu.VMEM((NY, COLS, NODES), BF),
            pltpu.VMEM((4, NX, COLS, 384), BF),
            pltpu.VMEM((4, NX, 80, 384), BF),
            pltpu.VMEM((80, NODES), BF),
            pltpu.VMEM((3, 512, 4096), BF),
            pltpu.VMEM((3, 32, 128), I32),
            pltpu.VMEM((3, 32, 128), F32),
            pltpu.VMEM((80, NODES), F32),
            pltpu.VMEM((NF, COLS, 128), BF),
            pltpu.VMEM((NF, COLS, 128), BF),
            pltpu.VMEM((NF, COLS, 128), BF),
            pltpu.VMEM((128, HID), F32),
            pltpu.VMEM((CPAD, HID), BF),
            pltpu.VMEM((CPAD, HID), BF),
            pltpu.VMEM((256, NODES), BF),
            pltpu.VMEM((1024, NODES), BF),
            pltpu.VMEM((128, 1024), BF),
            pltpu.VMEM((1024, 256), BF),
            pltpu.VMEM((1024, 256), BF),
            pltpu.VMEM((8, 128), F32),
            pltpu.VMEM((36, 80, 128), F32),
            pltpu.VMEM((128, NODES), BF),
            dma((3,)),
            dma((NY, 2)), dma((NY, 2)),
            dma((NY,)), dma((NY,)),
            dma((NF,)), dma((NF,)),
            dma((4, NX)), dma((4, NX)),
            dma((NF,)), dma((NF,)),
            dma((2, 6)), dma((2, 6)),
            dma, dma,
        ],
        compiler_params=pltpu.CompilerParams(
            collective_id=0, has_side_effects=True, vmem_limit_bytes=56 * 1024 * 1024
        ),
    )(
        tile_ids[0].T,
        jnp.transpose(counts, (2, 0, 1)),
        jnp.transpose(sources[0], (1, 2, 0)),
        jnp.transpose(targets[0], (1, 2, 0)),
        jnp.transpose(edge_weight[0], (1, 2, 0)),
        features[0].T,
        tiles[0],
        self_one,
        neigh_one,
        self_out.T,
        neigh_out.T,
    )
    return hidden[None], logits[None]


def solution(mesh):
    placed = (
        P("dom", None, "feat"),
        P("dom", None, None, None),
        P("dom", None, None),
        P("dom", None, None, None),
        P("dom", None, None, None),
        P("dom", None, None),
        P("dom", None, None, None),
        P(),
        P(),
        P(),
        P(),
    )
    return jax.shard_map(
        on_device,
        mesh=mesh,
        in_specs=placed,
        out_specs=(P("dom", "feat", None), P("dom", None, "feat")),
        check_vma=False,
    )
```

time: 322 us -> 111 us (0.34)
  waiting for transfers between devices: 130 us -> 0 us
  Pallas kernels: 0 us -> 107 us
  local copies, waits for them, and re-layouts: 72 us -> 3.27 us
  starting transfers between devices: 52.9 us -> 0 us
  other arithmetic: 25.9 us -> 0 us
  matrix products: 24.7 us -> 0 us
  between operations: 14.3 us -> 0.64 us
    pallas_call x0 -> x1, Pallas kernels: none -> 107 us  [on_device(): pl.pallas_call(kernel, out_shape=(jax.ShapeDtypeStruct((128, HID), BF), j...]
    all_to_all x4 -> x0, waiting for transfers between devices: 80.3 us -> none  [the longest x1 40.6 us: on_device(): lax.all_to_all(chosen, 'dom', split_axis=0, concat_axis=0, tiled=True)]
    gather x3 -> x0, local copies, waits for them, and re-layouts: 53.6 us -> none  [the longest x1 43.7 us: on_device(): outgoing = jnp.take(feature_cols, sources[0], axis=0)]
    all_to_all x4 -> x0, starting transfers between devices: 52.9 us -> none  [the longest x1 17.1 us: on_device(): lax.all_to_all(chosen, 'dom', split_axis=0, concat_axis=0, tiled=True)]
    all_gather x1 -> x0, waiting for transfers between devices: 49.4 us -> none  [on_device(): received = lax.all_gather(hidden, 'feat', axis=0, tiled=True)]
    dot_general x11 -> x0, matrix products: 24.7 us -> none  [the longest x1 9.98 us: on_device(): jnp.einsum('dgsr,dgsc->grc', edge_matrices, incoming, preferred_element_t...]
    select_n x6 -> x0, other arithmetic: 18.9 us -> none  [the longest x2 7.99 us: on_device(): outgoing = jnp.take(feature_cols, sources[0], axis=0)]
    unnamed x31 -> x2, local copies, waits for them, and re-layouts: 14.5 us -> 3.27 us
  transfers between devices with their start and end apart: 5 -> 0, of which waited for: 4 -> 0; matrix products, arithmetic and copies ran while one was open for 13% -> 0% of each run, Pallas kernels for 0% -> 0%
where the time goes in v1:
time: 111 us
  Pallas kernels  107 us (96%)
  local copies, waits for them, and re-layouts  3.27 us (3%)
    pallas_call x1, Pallas kernels, on_device(): pl.pallas_call(kernel, out_shape=(jax.ShapeDtypeStruct((128, HID), BF), j...  107 us
    unnamed x2, local copies, waits for them, and re-layouts  3.27 us

profile of v1, /device:TPU:1, one launch (start us, length us, event | category | flops | bytes accessed | tf_op | source)
XLA Modules:
  0.0 110.7 jit_solution(8581920385692248683)
XLA Ops:
  0.6 106.8 %shard_map.122 = (bf16[128,1024]{1,0:T(8,128)(2,1)}, f32[153,128]{1,0:T(8,128)}) custom-call(s32[2,36]{1,0:T(2,128)} %bitcast.31, s32[12,1,64]{2,1,0:T(1,128)} %bitcast.30, s32[12,16,64]{2,1,0:T(8,128)} %bitcast.26, s32[12,16,64]{2,1,0:T(8,128)} %bitcast.27, bf16[12,16,64]{2,1,0:T(8,128)(2,1)} %bitcast.29, bf16[64,1536]{1,0:T(8,128)(2,1)} %bitcast.25, ...), custom_call_target="tpu_custom_call" | custom-call | tf_op jit(solution)/shard_map/pallas_call | solution.py:396
  107.4 1.6 %copy.13 = f32[1,153,128]{2,0,1:T(1,128)} copy(f32[1,153,128]{2,1,0:T(8,128)} %bitcast.28) | data formatting | bytes 156672
  109.0 1.7 %copy.15 = bf16[1,128,1024]{2,1,0:T(8,128)(2,1)} copy(bf16[1,128,1024]{2,1,0:T(8,128)(2,1)} %bitcast.24) | data formatting | bytes 524288

commit v2 on v1

--- a/solution.py
+++ b/solution.py
@@ -135,12 +135,11 @@
     frows[f] = feat[:, pl.ds(pl.multiple_of(f * 128, 128), 128)]
 
     def gather(slot):
-        @pl.loop(0, 6)
-        def _(r):
-            here = table(slot)
+        here = table(slot)
+        for r in range(6):
             wide = jnp.concatenate([here[:, k * 256 : k * 256 + 256] for k in range(6)], axis=0)
             pick = jnp.concatenate(
-                [idx_in[slot, pl.ds(2 * r, 1), :], idx_in[slot, pl.ds(2 * r + 1, 1), :]], axis=1
+                [idx_in[slot, 2 * r : 2 * r + 1, :], idx_in[slot, 2 * r + 1 : 2 * r + 2, :]], axis=1
             )
             low = pick & 255
             high = pick >> 8
@@ -149,25 +148,39 @@
             kept = jnp.zeros((COLS, 256), F32)
             for k in range(6):
                 kept = jnp.where(high == k, got[k * COLS : k * COLS + COLS], kept)
-            picked[slot, :, pl.ds(pl.multiple_of(r * 256, 256), 256)] = kept.astype(BF)
+            picked[slot, :, r * 256 : r * 256 + 256] = kept.astype(BF)
 
     first_half = iota((COLS, 128), 1) < 64
 
+    def merge(b, q):
+        even, odd = PAIRS[b]
+        for col in range(4):
+            at = (q * 4 + col) * 128
+            one = picked[even, :, at : at + 128]
+            two = picked[odd, :, at : at + 128]
+            out1[b, 2 * col, :, q * 128 : q * 128 + 128] = jnp.where(first_half, one, two)
+            out1[b, 2 * col + 1, :, q * 128 : q * 128 + 128] = jnp.where(first_half, two, one)
+
     def merge_and_send(b):
-        even, odd = PAIRS[b]
         for q in range(3):
-            for col in range(4):
-                at = (q * 4 + col) * 128
-                one = picked[even, :, at : at + 128]
-                two = picked[odd, :, at : at + 128]
-                out1[b, 2 * col, :, q * 128 : q * 128 + 128] = jnp.where(first_half, one, two)
-                out1[b, 2 * col + 1, :, q * 128 : q * 128 + 128] = jnp.where(first_half, two, one)
+            merge(b, q)
         for k in (4, 3, 5, 2, 6, 1, 7):
             to = mod(xc + k, NX)
             go(remote(
                 out1.at[b, to], in1.at[b, xc, pl.ds(0, COLS)], xsend.at[b, k], xrecv.at[b, k], f, y * NX + to
             ))
         in1[b, xc, 0:COLS] = out1[b, xc]
+
+    def last_batch(q):
+        merge(3, q)
+        part = pl.ds(q * 128, 128)
+        for k in (4, 3, 5, 2, 6, 1, 7):
+            to = mod(xc + k, NX)
+            go(remote(
+                out1.at[3, to, :, part], in1.at[3, xc, pl.ds(0, COLS), part],
+                xsend.at[3 + q, k], xrecv.at[3 + q, k], f, y * NX + to,
+            ))
+        in1[3, xc, 0:COLS, part] = out1[3, xc, :, part]
 
     gather(0)
 
@@ -206,36 +219,63 @@
                     iota((512, 128), 0) == t, w, 0.0
                 ).astype(BF)
 
-    def scatter(b):
+    def scatter_part(b, q):
+        rows = jnp.concatenate([in1[b, i, :, q * 128 : q * 128 + 128] for i in range(NX)], axis=1)
+        acc[:, q * 512 : q * 512 + 512] += dot_nt(rows, scat[q, :, b * 1024 : b * 1024 + 1024])
+
+    def arrive_batch(b):
         for k in range(1, NX):
             arrived(in1.at[b, mod(xc + NX - k, NX), pl.ds(0, COLS)], xrecv.at[b, k])
+
+    def scatter(b):
+        arrive_batch(b)
         for q in range(3):
-            rows = jnp.concatenate([in1[b, i, :, q * 128 : q * 128 + 128] for i in range(NX)], axis=1)
-            acc[:, q * 512 : q * 512 + 512] += dot_nt(rows, scat[q, :, b * 1024 : b * 1024 + 1024])
+            scatter_part(b, q)
 
     build(0)
+    build(1)
     in1[:, :, COLS:80, :] = jnp.ones((4, NX, 16, 384), BF)
+    z[CPAD:256] = jnp.zeros((256 - CPAD, NODES), BF)
     ftd[0:COLS] = feat[...]
     ftd[COLS:80] = jnp.ones((16, NODES), BF)
 
-    for half in range(2):
-        took(1, half)
-        pass_on(1, 2, half, up)
-        took(7, half)
-        pass_on(7, 6, half, down)
+    took(1, 0)
+    pass_on(1, 2, 0, up)
+    took(7, 0)
+    pass_on(7, 6, 0, down)
+    build(2)
+    took(1, 1)
+    pass_on(1, 2, 1, up)
+    took(7, 1)
+    pass_on(7, 6, 1, down)
     arrived(idx_in.at[1], irecv.at[1])
     gather(1)
     merge_and_send(0)
+    loads[0].wait()
+
+    @pl.loop(0, 6)
+    def _(r):
+        for i in range(6):
+            t = r * 6 + i
+            cols = jnp.zeros((80, 128), BF)
+            for q in range(NF):
+                cols = jnp.where(ids[1, t] == q, ftd[:, q * 128 : q * 128 + 128], cols)
+            prod[t] = dot_nt(cols, tiles[t])
+
+    took(2, 0)
+    pass_on(2, 3, 0, up)
+    took(6, 0)
+    pass_on(6, 5, 0, down)
     arrived(idx_in.at[7], irecv.at[7])
     gather(7)
-    loads[0].wait()
-
-    @pl.loop(0, 36)
-    def _(t):
-        cols = jnp.zeros((80, 128), BF)
-        for q in range(NF):
-            cols = jnp.where(ids[1, t] == q, ftd[:, q * 128 : q * 128 + 128], cols)
-        prod[t] = dot_nt(cols, tiles[t])
+    build(3)
+    took(2, 1)
+    pass_on(2, 3, 1, up)
+    took(6, 1)
+    pass_on(6, 5, 1, down)
+    arrived(idx_in.at[2], irecv.at[2])
+    gather(2)
+    merge_and_send(1)
 
     @pl.loop(0, NF)
     def _(r):
@@ -244,24 +284,11 @@
             total = total + jnp.where(ids[0, t] == r, prod[t], 0.0)
         acc[:, pl.ds(pl.multiple_of(r * 128, 128), 128)] = total
 
-    for half in range(2):
-        took(2, half)
-        pass_on(2, 3, half, up)
-        took(6, half)
-        pass_on(6, 5, half, down)
-    arrived(idx_in.at[2], irecv.at[2])
-    gather(2)
-    merge_and_send(1)
-    arrived(idx_in.at[6], irecv.at[6])
-    gather(6)
-    build(1)
-    build(2)
-    build(3)
-    scatter(0)
-
     took(3, 0)
     pass_on(3, 4, 0, up)
     took(5, 0)
+    arrived(idx_in.at[6], irecv.at[6])
+    gather(6)
     took(3, 1)
     took(5, 1)
     pass_on(5, 4, 1, down)
@@ -270,24 +297,37 @@
     merge_and_send(2)
     arrived(idx_in.at[5], irecv.at[5])
     gather(5)
-
+    scatter(0)
+    took(4, 0)
+    took(4, 1)
+    arrived(idx_in.at[4], irecv.at[4])
+    gather(4)
+    for q in range(3):
+        last_batch(q)
+
+    scatter(1)
+    scatter(2)
     loads[1].wait()
     for k in range(1, NF):
         arrived(frows.at[mod(f + NF - k, NF)], frecv.at[k])
     pre[...] = dot(frows[...].reshape(768, 128).T, s1[...])
-
-    wso[CLS - 9 : CPAD] = jnp.zeros((16, HID), BF)
+    for q in range(3):
+        for k in range(1, NX):
+            arrived(in1.at[3, mod(xc + NX - k, NX), pl.ds(0, COLS), pl.ds(q * 128, 128)], xrecv.at[3 + q, k])
+        scatter_part(3, q)
+        for g in range(q * 4, q * 4 + 4):
+            part = acc[:, g * 128 : g * 128 + 128]
+            nsend_buf[g] = (part[0:COLS] / part[COLS : COLS + 1]).astype(BF)
+
+            @pl.when(f != g)
+            def _():
+                remote(nsend_buf.at[g], nrows.at[f], nsend.at[g], nrecv.at[f], g, d).start()
+
+    nrows[f] = nsend_buf[f]
+    deg[...] = acc[COLS : COLS + 8, pl.ds(pl.multiple_of(f * 128, 128), 128)]
+    loads[2].wait()
     wno[CLS - 9 : CPAD] = jnp.zeros((16, HID), BF)
-    wso[0:CLS] = so[...]
     wno[0:CLS] = no[...]
-
-    lane = iota((ND, 1024), 1)
-    spread = (lax.div(lane, 16) == iota((ND, 1024), 0)).astype(F32).astype(BF)
-    t2 = jnp.where(iota((16, ND), 0) < counts[f], targets[f], -512).astype(F32).astype(BF)
-    own = iota((16, 1024), 0) == (iota((16, 1024), 1) & 15)
-    t_row = jnp.sum(jnp.where(own, dot(t2, spread), 0.0), axis=0, keepdims=True).astype(I32)
-    w_row = jnp.sum(jnp.where(own, dot(weights[f], spread), 0.0), axis=0, keepdims=True)
-    scat2[...] = jnp.where(iota((128, 1024), 0) == t_row, w_row, 0.0).astype(BF)
     s2 = sources[f]
     high2 = (s2 >> 8).astype(F32).astype(BF)
     low2 = (s2 & 255).astype(F32).astype(BF)
@@ -304,6 +344,55 @@
                 (iota((128, 128), 1) + q * 128) == node
             ).astype(F32).astype(BF)
 
+    for k in range(1, NF):
+        g = mod(f + NF - k, NF)
+        arrived(nrows.at[g], nrecv.at[g])
+
+    hidden = jnp.maximum(pre[...] + dot(nrows[...].reshape(768, 128).T, n1[...]), 0.0).astype(BF)
+    hidden_ref[...] = hidden
+
+    def block_at(g):
+        return z.at[pl.ds(0, CPAD), pl.ds(pl.multiple_of(g * 128, 128), 128)]
+
+    z[0:CPAD, pl.ds(pl.multiple_of(f * 128, 128), 128)] = dot_nt(wno[...], hidden_ref[...]).astype(BF)
+
+    way = 1 - 2 * core
+    ways = (way, -way)
+
+    def from_far(side, k):
+        return block_at(mod(f + NF - ways[side] * k, NF))
+
+    def throw(side, held, hops):
+        block = from_far(side, held)
+        k = held + hops
+        go(remote(block, block, zsend.at[side, k], zrecv.at[side, k], mod(f + NF + ways[side] * hops, NF), d))
+
+    def caught(side, k):
+        arrived(from_far(side, k), zrecv.at[side, k])
+
+    for hops in (4, 2, 1):
+        for side in range(2):
+            throw(side, 0, hops)
+    caught(0, 4)
+    throw(0, 4, 2)
+    throw(0, 4, 1)
+    caught(1, 4)
+    throw(1, 4, 1)
+    for side in range(2):
+        caught(side, 2)
+        throw(side, 2, 1)
+
+    wso[CLS - 9 : CPAD] = jnp.zeros((16, HID), BF)
+    wso[0:CLS] = so[...]
+    own_term = dot_nt(wso[...], hidden_ref[...])
+    lane = iota((ND, 1024), 1)
+    spread = (lax.div(lane, 16) == iota((ND, 1024), 0)).astype(F32).astype(BF)
+    t2 = jnp.where(iota((16, ND), 0) < counts[f], targets[f], -512).astype(F32).astype(BF)
+    own = iota((16, 1024), 0) == (iota((16, 1024), 1) & 15)
+    t_row = jnp.sum(jnp.where(own, dot(t2, spread), 0.0), axis=0, keepdims=True).astype(I32)
+    w_row = jnp.sum(jnp.where(own, dot(weights[f], spread), 0.0), axis=0, keepdims=True)
+    scat2[...] = jnp.where(iota((128, 1024), 0) == t_row, w_row, 0.0).astype(BF)
+
     @pl.loop(0, NF)
     def _(q):
         block = jnp.zeros((128, 128), BF)
@@ -311,80 +400,45 @@
             block = jnp.where((ids[0, t] == f) & (ids[1, t] == q), tiles[t], block)
         band[:, pl.ds(pl.multiple_of(q * 128, 128), 128)] = block
 
-    z[...] = jnp.zeros((256, NODES), BF)
-    scatter(1)
-
-    took(4, 0)
-    took(4, 1)
-    arrived(idx_in.at[4], irecv.at[4])
-    gather(4)
-    merge_and_send(3)
-    scatter(2)
-    loads[2].wait()
-    scatter(3)
-
-    for k in range(NF):
-        g = mod(f + k, NF)
-        part = acc[:, pl.ds(pl.multiple_of(g * 128, 128), 128)]
-        mean = (part[0:COLS] / part[COLS : COLS + 1]).astype(BF)
-        if k == 0:
-            nrows[f] = mean
-            deg[...] = part[COLS : COLS + 8]
-        else:
-            nsend_buf[g] = mean
-            go(remote(nsend_buf.at[g], nrows.at[f], nsend.at[k], nrecv.at[k], g, d))
-    for k in range(1, NF):
-        arrived(nrows.at[mod(f + NF - k, NF)], nrecv.at[k])
-
-    hidden = jnp.maximum(pre[...] + dot(nrows[...].reshape(768, 128).T, n1[...]), 0.0).astype(BF)
-    hidden_ref[...] = hidden
-
-    def block_at(g):
-        return z.at[pl.ds(0, CPAD), pl.ds(pl.multiple_of(g * 128, 128), 128)]
-
-    z[0:CPAD, pl.ds(pl.multiple_of(f * 128, 128), 128)] = dot_nt(wno[...], hidden_ref[...]).astype(BF)
-
-    right = mod(f + 1, NF)
-    left = mod(f + NF - 1, NF)
-
-    def ring(side, k):
-        g = mod(f + NF - k, NF) if side == 0 else mod(f + k, NF)
-        go(remote(
-            block_at(g), block_at(g), zsend.at[side, k], zrecv.at[side, k], right if side == 0 else left, d
-        ))
-
-    ring(0, 0)
-    ring(1, 0)
-    own_term = dot_nt(wso[...], hidden_ref[...])
-    for k in range(6):
-        arrived(block_at(mod(f + NF - 1 - k, NF)), zrecv.at[0, k])
-        if k < 5:
-            ring(0, k + 1)
-            arrived(block_at(mod(f + 1 + k, NF)), zrecv.at[1, k])
-        if k < 4:
-            ring(1, k + 1)
+    for k in (1, 3, 5):
+        caught(0, k)
+        caught(1, k)
+    caught(0, 6)
 
     for j in range(4):
-        out2[j * 256 : j * 256 + 256] = dot_nt(oh2[j * 256 : j * 256 + 256], z[...]).astype(BF)
-
-    @pl.loop(1, ND)
-    def _(k):
-        to = mod(d + k, ND)
-        remote(
-            out2.at[pl.ds(pl.multiple_of(to * 16, 16), 16)], in2.at[pl.ds(pl.multiple_of(d * 16, 16), 16)],
-            asend, arecv, f, to,
-        ).start()
+        base = mod(lax.div(d, 16) + j, 4) * 16
+        rows = pl.ds(pl.multiple_of(base * 16, 256), 256)
+        out2[rows] = dot_nt(oh2[rows], z[...]).astype(BF)
+
+        @pl.loop(0, 16)
+        def _(k):
+            to = base + mod(d + k, 16)
+
+            @pl.when(to != d)
+            def _():
+                remote(
+                    out2.at[pl.ds(pl.multiple_of(to * 16, 16), 16)], in2.at[pl.ds(pl.multiple_of(d * 16, 16), 16)],
+                    asend, arecv, f, to,
+                ).start()
 
     mine = pl.ds(pl.multiple_of(d * 16, 16), 16)
     in2[mine] = out2[mine]
     total = dot_nt(band[...], z[...])
     arrived(in2.at[pl.ds(0, 1008)], arecv)
     total = total + dot(scat2[...], in2[...])
-    logits_ref[...] = own_term[0:CLS] + (total.T)[0:CLS] / deg[0:1]
+    logits_ref[:, 0, :] = own_term[0:CLS] + (total.T)[0:CLS] / deg[0:1]
 
     arrived(out2.at[pl.ds(0, 1008)], asend)
+    for k in range(1, NF):
+        g = mod(f + k, NF)
+        arrived(nsend_buf.at[g], nsend.at[g])
     for copy in sent:
         copy.wait_send()
+
+
+def hand_over(hidden_ref, logits_ref, hidden_out, logits_out):
+    hidden_out[...] = hidden_ref[...]
+    logits_out[...] = logits_ref[...]
 
 
 def on_device(
@@ -395,7 +449,7 @@
     dma = pltpu.SemaphoreType.DMA
     hidden, logits = pl.pallas_call(
         kernel,
-        out_shape=(jax.ShapeDtypeStruct((128, HID), BF), jax.ShapeDtypeStruct((CLS, 128), F32)),
+        out_shape=(jax.ShapeDtypeStruct((128, HID), BF), jax.ShapeDtypeStruct((CLS, 1, 128), F32)),
         in_specs=[pl.BlockSpec(memory_space=pltpu.SMEM)] + [vmem] * 5 + [anywhere] * 3 + [vmem] * 2,
         out_specs=(vmem, vmem),
         scratch_shapes=[
@@ -431,9 +485,9 @@
             dma((NY, 2)), dma((NY, 2)),
             dma((NY,)), dma((NY,)),
             dma((NF,)), dma((NF,)),
-            dma((4, NX)), dma((4, NX)),
+            dma((6, NX)), dma((6, NX)),
             dma((NF,)), dma((NF,)),
-            dma((2, 6)), dma((2, 6)),
+            dma((2, 7)), dma((2, 7)),
             dma, dma,
         ],
         compiler_params=pltpu.CompilerParams(
@@ -452,7 +506,13 @@
         self_out.T,
         neigh_out.T,
     )
-    return hidden[None], logits[None]
+    hidden, logits = pl.pallas_call(
+        hand_over,
+        out_shape=(jax.ShapeDtypeStruct((128, HID), BF), jax.ShapeDtypeStruct((CLS, 1, 128), F32)),
+        in_specs=[vmem] * 2,
+        out_specs=(vmem, vmem),
+    )(hidden, logits)
+    return hidden[None], jnp.transpose(logits, (1, 0, 2))
 
 
 def solution(mesh):

time: 111 us -> 93.2 us (0.84)
  Pallas kernels: 107 us -> 92.4 us
  local copies, waits for them, and re-layouts: 3.27 us -> 0 us
    pallas_call x1, Pallas kernels: 107 us -> 90.7 us  [on_device(): pl.pallas_call(kernel, out_shape=(jax.ShapeDtypeStruct((128, HID), BF), j...]
    unnamed x2 -> x0, local copies, waits for them, and re-layouts: 3.27 us -> none
    pallas_call x0 -> x1, Pallas kernels: none -> 1.7 us  [on_device(): pl.pallas_call(hand_over, out_shape=(jax.ShapeDtypeStruct((128, HID), BF)...]
where the time goes in v2:
time: 93.2 us; the launch traced here: 93 us
  Pallas kernels  92.4 us (99%)
    pallas_call x1, Pallas kernels, on_device(): pl.pallas_call(kernel, out_shape=(jax.ShapeDtypeStruct((128, HID), BF), j...  90.7 us

profile of v2, /device:TPU:1, one launch (start us, length us, event | category | flops | bytes accessed | tf_op | source)
XLA Modules:
  0.0 93.0 jit_solution(5173422548792788092)
XLA Ops:
  0.6 90.7 %shard_map.122 = (bf16[128,1024]{1,0:T(8,128)(2,1)}, f32[153,1,128]{2,1,0:T(1,128)}) custom-call(s32[2,36]{1,0:T(2,128)} %bitcast.29, s32[12,1,64]{2,1,0:T(1,128)} %bitcast.28, s32[12,16,64]{2,1,0:T(8,128)} %bitcast.25, s32[12,16,64]{2,1,0:T(8,128)} %bitcast.26, bf16[12,16,64]{2,1,0:T(8,128)(2,1)} %bitcast.27, bf16[64,1536]{1,0:T(8,128)(2,1)} %bitcast.24, ...), custom_call_target="tpu_custom_call" | custom-call | tf_op jit(solution)/shard_map/pallas_call | solution.py:450
  91.3 1.7 %shard_map.123 = (bf16[128,1024]{1,0:T(8,128)(2,1)}, f32[153,1,128]{2,1,0:T(1,128)}) custom-call(bf16[128,1024]{1,0:T(8,128)(2,1)} %get-tuple-element.6.hidden_ref, f32[153,1,128]{2,1,0:T(1,128)} %get-tuple-element.7.logits_ref), custom_call_target="tpu_custom_call" | custom-call | tf_op jit(solution)/shard_map/pallas_call | solution.py:509

commit v3 on v2

--- a/solution.py
+++ b/solution.py
@@ -40,25 +40,17 @@
 
 
 def kernel(
-    ids, counts, sources, targets, weights, feat, tiles_hbm, s1_hbm, n1_hbm, so, no,
+    ids, counts_hbm, sources_hbm, targets_hbm, weights_hbm, feat_hbm, tiles_hbm, s1_hbm, n1_hbm, so_hbm, no_hbm,
     hidden_ref, logits_ref,
-    tiles, s1, n1, tab, idx_out, idx_in, picked, out1, in1, ftd, scat, rows_t, rows_w, acc,
-    frows, nsend_buf, nrows, pre, wso, wno, z, oh2, scat2, out2, in2, deg, prod, band,
-    loc, tsend, trecv, isend, irecv, fsend, frecv, xsend, xrecv, nsend, nrecv, zsend, zrecv, asend, arecv,
+    counts, sources, targets, weights, feat, so, no, tiles, s1, n1, tab, idx_out, idx_in, picked, out1, in1, ftd, scat, rows_t, rows_w, acc,
+    frows, nsend_buf, nrows, pre, wso, wno, z, oh2, scat2, out2, in2, deg, prod, band, outb, inb, outb2, inb2,
+    loc, tsend, trecv, isend, irecv, fsend, frecv, xsend, xrecv, nsend, nrecv, zsend, zrecv, asend, arecv, bsend, brecv,
 ):
     f = lax.axis_index("feat")
     d = lax.axis_index("dom")
     y = lax.div(d, jnp.int32(NX))
     xc = mod(d, NX)
     core = mod(d, 2)
-
-    loads = [
-        pltpu.make_async_copy(tiles_hbm, tiles, loc.at[0]),
-        pltpu.make_async_copy(s1_hbm, s1, loc.at[1]),
-        pltpu.make_async_copy(n1_hbm, n1, loc.at[2]),
-    ]
-    for load in loads:
-        load.start()
 
     def remote(src, dst, ss, rs, fi, di):
         return pltpu.make_async_remote_copy(
@@ -82,7 +74,20 @@
     for k in range(1, NF):
         pl.semaphore_signal(barrier, inc=1, device_id=(mod(f + k, NF), d), device_id_type=MESH)
 
-    src = sources[...].reshape(192, ND)
+    loads = [
+        pltpu.make_async_copy(far, near, loc.at[i])
+        for i, (far, near) in enumerate((
+            (sources_hbm, sources), (feat_hbm, feat), (targets_hbm, targets), (counts_hbm, counts),
+            (weights_hbm, weights), (tiles_hbm, tiles), (s1_hbm, s1), (n1_hbm, n1), (no_hbm, no), (so_hbm, so),
+        ))
+    ]
+    for load in loads:
+        load.start()
+
+    spread_out = [place * 3 + third for third in range(3) for place in range(4)]
+
+    loads[0].wait()
+    src = jnp.concatenate([sources[g] for g in spread_out], axis=0)
     both = jnp.concatenate([src >> 8, src & 255], axis=0).astype(F32).astype(BF)
     r32 = iota((32, ND), 0)
     e32 = iota((32, ND), 1)
@@ -98,6 +103,7 @@
             idx_out[row, q * 4 : q * 4 + 4, :] = tile[row * 4 : row * 4 + 4]
     idx_in[0] = idx_out[y]
 
+    loads[1].wait()
     pl.semaphore_wait(barrier, NY - 1 + NX - 1 + NF - 1)
 
     sent = []
@@ -184,9 +190,12 @@
 
     gather(0)
 
-    live = iota((NF, 16, ND), 1) < counts[...]
-    t_all = jnp.where(live, targets[...], -512).reshape(192, ND)
-    w_all = weights[...].reshape(192, ND)
+    for i in (2, 3, 4):
+        loads[i].wait()
+    t_all = jnp.concatenate(
+        [jnp.where(iota((16, ND), 0) < counts[g], targets[g], -512) for g in spread_out], axis=0
+    )
+    w_all = jnp.concatenate([weights[g] for g in spread_out], axis=0)
     both = jnp.concatenate([t_all.astype(F32).astype(BF), w_all], axis=0)
     batch = lax.div(r32, 8)
     halves = []
@@ -251,7 +260,7 @@
     arrived(idx_in.at[1], irecv.at[1])
     gather(1)
     merge_and_send(0)
-    loads[0].wait()
+    loads[5].wait()
 
     @pl.loop(0, 6)
     def _(r):
@@ -278,11 +287,12 @@
     merge_and_send(1)
 
     @pl.loop(0, NF)
-    def _(r):
+    def _(p):
+        r = mod(p, 4) * 3 + lax.div(p, 4)
         total = jnp.zeros((80, 128), F32)
         for t in range(36):
             total = total + jnp.where(ids[0, t] == r, prod[t], 0.0)
-        acc[:, pl.ds(pl.multiple_of(r * 128, 128), 128)] = total
+        acc[:, pl.ds(pl.multiple_of(p * 128, 128), 128)] = total
 
     took(3, 0)
     pass_on(3, 4, 0, up)
@@ -307,7 +317,7 @@
 
     scatter(1)
     scatter(2)
-    loads[1].wait()
+    loads[6].wait()
     for k in range(1, NF):
         arrived(frows.at[mod(f + NF - k, NF)], frecv.at[k])
     pre[...] = dot(frows[...].reshape(768, 128).T, s1[...])
@@ -315,8 +325,10 @@
         for k in range(1, NX):
             arrived(in1.at[3, mod(xc + NX - k, NX), pl.ds(0, COLS), pl.ds(q * 128, 128)], xrecv.at[3 + q, k])
         scatter_part(3, q)
-        for g in range(q * 4, q * 4 + 4):
-            part = acc[:, g * 128 : g * 128 + 128]
+        for i in range(4):
+            place = mod(lax.div(f, 3) + i, 4)
+            g = place * 3 + q
+            part = acc[:, pl.ds(pl.multiple_of(q * 512 + place * 128, 128), 128)]
             nsend_buf[g] = (part[0:COLS] / part[COLS : COLS + 1]).astype(BF)
 
             @pl.when(f != g)
@@ -324,8 +336,9 @@
                 remote(nsend_buf.at[g], nrows.at[f], nsend.at[g], nrecv.at[f], g, d).start()
 
     nrows[f] = nsend_buf[f]
-    deg[...] = acc[COLS : COLS + 8, pl.ds(pl.multiple_of(f * 128, 128), 128)]
-    loads[2].wait()
+    deg[...] = acc[COLS : COLS + 8, pl.ds(pl.multiple_of(mod(f, 3) * 512 + lax.div(f, 3) * 128, 128), 128)]
+    loads[7].wait()
+    loads[8].wait()
     wno[CLS - 9 : CPAD] = jnp.zeros((16, HID), BF)
     wno[0:CLS] = no[...]
     s2 = sources[f]
@@ -382,6 +395,7 @@
         caught(side, 2)
         throw(side, 2, 1)
 
+    loads[9].wait()
     wso[CLS - 9 : CPAD] = jnp.zeros((16, HID), BF)
     wso[0:CLS] = so[...]
     own_term = dot_nt(wso[...], hidden_ref[...])
@@ -406,27 +420,51 @@
     caught(0, 6)
 
     for j in range(4):
-        base = mod(lax.div(d, 16) + j, 4) * 16
-        rows = pl.ds(pl.multiple_of(base * 16, 256), 256)
-        out2[rows] = dot_nt(oh2[rows], z[...]).astype(BF)
-
-        @pl.loop(0, 16)
-        def _(k):
-            to = base + mod(d + k, 16)
-
-            @pl.when(to != d)
-            def _():
-                remote(
-                    out2.at[pl.ds(pl.multiple_of(to * 16, 16), 16)], in2.at[pl.ds(pl.multiple_of(d * 16, 16), 16)],
-                    asend, arecv, f, to,
-                ).start()
+        got = dot_nt(oh2[j * 256 : j * 256 + 256], z[...])
+        out2[j * 256 : j * 256 + 256] = got[:, 0:128].astype(BF)
+        rest = got[:, 128:160]
+        for half in range(2):
+            outb[j * 2 + half] = jnp.concatenate(
+                [rest[(half * 8 + i) * 16 : (half * 8 + i) * 16 + 16] for i in range(NX)], axis=1
+            ).astype(BF)
+    for k in range(1, NY):
+        to = mod(y + k, NY)
+        go(remote(outb.at[to], inb.at[y], bsend.at[0, k], brecv.at[0, k], f, to * NX + xc))
+    inb[y] = outb[y]
+
+    @pl.loop(1, ND)
+    def _(k):
+        to = mod(d + k, ND)
+        remote(
+            out2.at[pl.ds(pl.multiple_of(to * 16, 16), 16)], in2.at[pl.ds(pl.multiple_of(d * 16, 16), 16)],
+            asend, arecv, f, to,
+        ).start()
 
     mine = pl.ds(pl.multiple_of(d * 16, 16), 16)
     in2[mine] = out2[mine]
     total = dot_nt(band[...], z[...])
+
+    for k in range(1, NY):
+        arrived(inb.at[mod(y + NY - k, NY)], brecv.at[0, k])
+    for i in range(NX):
+        outb2[i] = jnp.concatenate(
+            [inb[r, :, i * 32 : i * 32 + 32].astype(F32) for r in range(NY)], axis=1
+        ).astype(BF)
+    for k in range(1, NX):
+        to = mod(xc + k, NX)
+        go(remote(outb2.at[to], inb2.at[xc], bsend.at[1, k], brecv.at[1, k], f, y * NX + to))
+    inb2[xc] = outb2[xc]
+    for k in range(1, NX):
+        arrived(inb2.at[mod(xc + NX - k, NX)], brecv.at[1, k])
+    flat = inb2[...].reshape(128, 256).astype(F32)
+    flat = jnp.concatenate([flat[:, r * 32 : r * 32 + 32] for r in range(NY)], axis=0).astype(BF)
+    few = dot(scat2[...], flat)
+    total_b = total[:, 128:256] + jnp.concatenate([few, jnp.zeros((128, 96), F32)], axis=1)
+    logits_ref[128:CLS, 0, :] = own_term[128:CLS] + (total_b.T)[0 : CLS - 128] / deg[0:1]
+
     arrived(in2.at[pl.ds(0, 1008)], arecv)
-    total = total + dot(scat2[...], in2[...])
-    logits_ref[:, 0, :] = own_term[0:CLS] + (total.T)[0:CLS] / deg[0:1]
+    total_a = total[:, 0:128] + dot(scat2[...], in2[...])
+    logits_ref[0:128, 0, :] = own_term[0:128] + total_a.T / deg[0:1]
 
     arrived(out2.at[pl.ds(0, 1008)], asend)
     for k in range(1, NF):
@@ -450,9 +488,16 @@
     hidden, logits = pl.pallas_call(
         kernel,
         out_shape=(jax.ShapeDtypeStruct((128, HID), BF), jax.ShapeDtypeStruct((CLS, 1, 128), F32)),
-        in_specs=[pl.BlockSpec(memory_space=pltpu.SMEM)] + [vmem] * 5 + [anywhere] * 3 + [vmem] * 2,
+        in_specs=[pl.BlockSpec(memory_space=pltpu.SMEM)] + [anywhere] * 10,
         out_specs=(vmem, vmem),
         scratch_shapes=[
+            pltpu.VMEM((NF, 1, ND), I32),
+            pltpu.VMEM((NF, 16, ND), I32),
+            pltpu.VMEM((NF, 16, ND), I32),
+            pltpu.VMEM((NF, 16, ND), BF),
+            pltpu.VMEM((COLS, NODES), BF),
+            pltpu.VMEM((CLS, HID), BF),
+            pltpu.VMEM((CLS, HID), BF),
             pltpu.VMEM((36, 128, 128), BF),
             pltpu.VMEM((768, HID), BF),
             pltpu.VMEM((768, HID), BF),
@@ -476,12 +521,16 @@
             pltpu.VMEM((256, NODES), BF),
             pltpu.VMEM((1024, NODES), BF),
             pltpu.VMEM((128, 1024), BF),
-            pltpu.VMEM((1024, 256), BF),
-            pltpu.VMEM((1024, 256), BF),
+            pltpu.VMEM((1024, 128), BF),
+            pltpu.VMEM((1024, 128), BF),
             pltpu.VMEM((8, 128), F32),
             pltpu.VMEM((36, 80, 128), F32),
             pltpu.VMEM((128, NODES), BF),
-            dma((3,)),
+            pltpu.VMEM((NY, 16, 256), BF),
+            pltpu.VMEM((NY, 16, 256), BF),
+            pltpu.VMEM((NY, 16, 256), BF),
+            pltpu.VMEM((NY, 16, 256), BF),
+            dma((10,)),
             dma((NY, 2)), dma((NY, 2)),
             dma((NY,)), dma((NY,)),
             dma((NF,)), dma((NF,)),
@@ -489,6 +538,7 @@
             dma((NF,)), dma((NF,)),
             dma((2, 7)), dma((2, 7)),
             dma, dma,
+            dma((2, 8)), dma((2, 8)),
         ],
         compiler_params=pltpu.CompilerParams(
             collective_id=0, has_side_effects=True, vmem_limit_bytes=56 * 1024 * 1024

time: 93.2 us -> 87.4 us (0.938)
  Pallas kernels: 92.4 us -> 86.6 us
    pallas_call x1, Pallas kernels: 90.7 us -> 84.9 us  [on_device(): pl.pallas_call(kernel, out_shape=(jax.ShapeDtypeStruct((128, HID), BF), j...]
where the time goes in v3:
time: 87.4 us; the launch traced here: 87.2 us
  Pallas kernels  86.6 us (99%)
    pallas_call x1, Pallas kernels, on_device(): pl.pallas_call(kernel, out_shape=(jax.ShapeDtypeStruct((128, HID), BF), j...  84.9 us

profile of v3, /device:TPU:1, one launch (start us, length us, event | category | flops | bytes accessed | tf_op | source)
XLA Modules:
  0.0 87.2 jit_solution(8239901406188122830)
XLA Ops:
  0.6 84.9 %shard_map.122 = (bf16[128,1024]{1,0:T(8,128)(2,1)}, f32[153,1,128]{2,1,0:T(1,128)}) custom-call(s32[2,36]{1,0:T(2,128)} %bitcast.29, s32[12,1,64]{2,1,0:T(1,128)} %bitcast.28, s32[12,16,64]{2,1,0:T(8,128)} %bitcast.25, s32[12,16,64]{2,1,0:T(8,128)} %bitcast.26, bf16[12,16,64]{2,1,0:T(8,128)(2,1)} %bitcast.27, bf16[64,1536]{1,0:T(8,128)(2,1)} %bitcast.24, ...), custom_call_target="tpu_custom_call" | custom-call | tf_op jit(solution)/shard_map/pallas_call | solution.py:488
  85.5 1.7 %shard_map.123 = (bf16[128,1024]{1,0:T(8,128)(2,1)}, f32[153,1,128]{2,1,0:T(1,128)}) custom-call(bf16[128,1024]{1,0:T(8,128)(2,1)} %get-tuple-element.6.hidden_ref, f32[153,1,128]{2,1,0:T(1,128)} %get-tuple-element.7.logits_ref), custom_call_target="tpu_custom_call" | custom-call | tf_op jit(solution)/shard_map/pallas_call | solution.py:559

commit v4 on v3

--- a/solution.py
+++ b/solution.py
@@ -9,6 +9,7 @@
 BF = jnp.bfloat16
 F32 = jnp.float32
 I32 = jnp.int32
+I16 = jnp.int16
 NT = (((1,), (1,)), ((), ()))
 
 NF = 12
@@ -97,10 +98,13 @@
         pick = (e32 == r32 * 2 + (flip ^ h)).astype(F32).astype(BF)
         got = dot_nt(pick, both)
         halves.append((got[:, :192] * 256.0 + got[:, 192:]).astype(I32))
-    for q in range(3):
-        tile = jnp.concatenate([halves[0][:, q * 64 : q * 64 + 64], halves[1][:, q * 64 : q * 64 + 64]], axis=1)
-        for row in range(NY):
-            idx_out[row, q * 4 : q * 4 + 4, :] = tile[row * 4 : row * 4 + 4]
+    thirds = [
+        jnp.concatenate([halves[0][:, q * 64 : q * 64 + 64], halves[1][:, q * 64 : q * 64 + 64]], axis=1)
+        for q in range(3)
+    ]
+    for row in range(NY):
+        some = [third[row * 4 : row * 4 + 4] for third in thirds] + [jnp.zeros((4, 128), I32)]
+        idx_out[row] = jnp.concatenate(some, axis=0).astype(I16)
     idx_in[0] = idx_out[y]
 
     loads[1].wait()
@@ -116,14 +120,14 @@
         return feat if slot == 0 else tab.at[slot]
 
     def pass_on(from_slot, to_slot, half, di):
-        part = pl.ds(half * 768, 768)
+        part = pl.ds(half * 32, 32)
         go(remote(
-            table(from_slot).at[:, part], tab.at[to_slot, :, part],
+            table(from_slot).at[part], tab.at[to_slot, part],
             tsend.at[to_slot, half], trecv.at[to_slot, half], f, di,
         ))
 
     def took(slot, half):
-        arrived(tab.at[slot, :, pl.ds(half * 768, 768)], trecv.at[slot, half])
+        arrived(tab.at[slot, pl.ds(half * 32, 32)], trecv.at[slot, half])
 
     up = row_peer(1)
     down = row_peer(NY - 1)
@@ -140,21 +144,21 @@
         ))
     frows[f] = feat[:, pl.ds(pl.multiple_of(f * 128, 128), 128)]
 
-    def gather(slot):
+    def gather(slot, half):
         here = table(slot)
+        rows = slice(half * 32, half * 32 + 32)
+        ids_here = idx_in[slot].astype(I32)
         for r in range(6):
-            wide = jnp.concatenate([here[:, k * 256 : k * 256 + 256] for k in range(6)], axis=0)
-            pick = jnp.concatenate(
-                [idx_in[slot, 2 * r : 2 * r + 1, :], idx_in[slot, 2 * r + 1 : 2 * r + 2, :]], axis=1
-            )
+            wide = jnp.concatenate([here[rows, k * 256 : k * 256 + 256] for k in range(6)], axis=0)
+            pick = jnp.concatenate([ids_here[2 * r : 2 * r + 1], ids_here[2 * r + 1 : 2 * r + 2]], axis=1)
             low = pick & 255
             high = pick >> 8
             one_hot = (iota((256, 256), 0) == low).astype(F32).astype(BF)
             got = dot(wide, one_hot)
-            kept = jnp.zeros((COLS, 256), F32)
+            kept = jnp.zeros((32, 256), F32)
             for k in range(6):
-                kept = jnp.where(high == k, got[k * COLS : k * COLS + COLS], kept)
-            picked[slot, :, r * 256 : r * 256 + 256] = kept.astype(BF)
+                kept = jnp.where(high == k, got[k * 32 : k * 32 + 32], kept)
+            picked[slot, rows, r * 256 : r * 256 + 256] = kept.astype(BF)
 
     first_half = iota((COLS, 128), 1) < 64
 
@@ -167,15 +171,24 @@
             out1[b, 2 * col, :, q * 128 : q * 128 + 128] = jnp.where(first_half, one, two)
             out1[b, 2 * col + 1, :, q * 128 : q * 128 + 128] = jnp.where(first_half, two, one)
 
-    def merge_and_send(b):
+    def merge_and_send(b, half):
+        even, odd = PAIRS[b]
+        rows = slice(half * 32, half * 32 + 32)
         for q in range(3):
-            merge(b, q)
+            for col in range(4):
+                at = (q * 4 + col) * 128
+                one = picked[even, rows, at : at + 128]
+                two = picked[odd, rows, at : at + 128]
+                out1[b, 2 * col, rows, q * 128 : q * 128 + 128] = jnp.where(first_half[rows], one, two)
+                out1[b, 2 * col + 1, rows, q * 128 : q * 128 + 128] = jnp.where(first_half[rows], two, one)
+        part = pl.ds(half * 32, 32)
         for k in (4, 3, 5, 2, 6, 1, 7):
             to = mod(xc + k, NX)
             go(remote(
-                out1.at[b, to], in1.at[b, xc, pl.ds(0, COLS)], xsend.at[b, k], xrecv.at[b, k], f, y * NX + to
+                out1.at[b, to, part], in1.at[b, xc, part],
+                xsend.at[b * 2 + half, k], xrecv.at[b * 2 + half, k], f, y * NX + to,
             ))
-        in1[b, xc, 0:COLS] = out1[b, xc]
+        in1[b, xc, rows] = out1[b, xc, rows]
 
     def last_batch(q):
         merge(3, q)
@@ -184,11 +197,12 @@
             to = mod(xc + k, NX)
             go(remote(
                 out1.at[3, to, :, part], in1.at[3, xc, pl.ds(0, COLS), part],
-                xsend.at[3 + q, k], xrecv.at[3 + q, k], f, y * NX + to,
+                xsend.at[6 + q, k], xrecv.at[6 + q, k], f, y * NX + to,
             ))
         in1[3, xc, 0:COLS, part] = out1[3, xc, :, part]
 
-    gather(0)
+    gather(0, 0)
+    gather(0, 1)
 
     for i in (2, 3, 4):
         loads[i].wait()
@@ -234,12 +248,23 @@
 
     def arrive_batch(b):
         for k in range(1, NX):
-            arrived(in1.at[b, mod(xc + NX - k, NX), pl.ds(0, COLS)], xrecv.at[b, k])
+            for half in range(2):
+                arrived(in1.at[b, mod(xc + NX - k, NX), pl.ds(half * 32, 32)], xrecv.at[b * 2 + half, k])
 
     def scatter(b):
         arrive_batch(b)
         for q in range(3):
             scatter_part(b, q)
+
+    def multiply(low, high):
+        @pl.loop(low, high)
+        def _(r):
+            for i in range(6):
+                t = r * 6 + i
+                cols = jnp.zeros((80, 128), BF)
+                for q in range(NF):
+                    cols = jnp.where(ids[1, t] == q, ftd[:, q * 128 : q * 128 + 128], cols)
+                prod[t] = dot_nt(cols, tiles[t])
 
     build(0)
     build(1)
@@ -252,39 +277,62 @@
     pass_on(1, 2, 0, up)
     took(7, 0)
     pass_on(7, 6, 0, down)
-    build(2)
+    arrived(idx_in.at[1], irecv.at[1])
+    gather(1, 0)
+    merge_and_send(0, 0)
     took(1, 1)
     pass_on(1, 2, 1, up)
     took(7, 1)
     pass_on(7, 6, 1, down)
-    arrived(idx_in.at[1], irecv.at[1])
-    gather(1)
-    merge_and_send(0)
+    gather(1, 1)
+    merge_and_send(0, 1)
+    arrived(idx_in.at[7], irecv.at[7])
+    gather(7, 0)
     loads[5].wait()
-
-    @pl.loop(0, 6)
-    def _(r):
-        for i in range(6):
-            t = r * 6 + i
-            cols = jnp.zeros((80, 128), BF)
-            for q in range(NF):
-                cols = jnp.where(ids[1, t] == q, ftd[:, q * 128 : q * 128 + 128], cols)
-            prod[t] = dot_nt(cols, tiles[t])
+    multiply(0, 3)
 
     took(2, 0)
     pass_on(2, 3, 0, up)
     took(6, 0)
     pass_on(6, 5, 0, down)
-    arrived(idx_in.at[7], irecv.at[7])
-    gather(7)
-    build(3)
+    arrived(idx_in.at[2], irecv.at[2])
+    gather(2, 0)
+    merge_and_send(1, 0)
+    gather(7, 1)
     took(2, 1)
     pass_on(2, 3, 1, up)
     took(6, 1)
     pass_on(6, 5, 1, down)
-    arrived(idx_in.at[2], irecv.at[2])
-    gather(2)
-    merge_and_send(1)
+    gather(2, 1)
+    merge_and_send(1, 1)
+    build(2)
+    arrived(idx_in.at[6], irecv.at[6])
+    gather(6, 0)
+
+    took(3, 0)
+    pass_on(3, 4, 0, up)
+    took(5, 0)
+    arrived(idx_in.at[3], irecv.at[3])
+    gather(3, 0)
+    merge_and_send(2, 0)
+    gather(6, 1)
+    took(3, 1)
+    took(5, 1)
+    pass_on(5, 4, 1, down)
+    gather(3, 1)
+    merge_and_send(2, 1)
+    arrived(idx_in.at[5], irecv.at[5])
+    gather(5, 0)
+    gather(5, 1)
+    build(3)
+    multiply(3, 6)
+    took(4, 0)
+    arrived(idx_in.at[4], irecv.at[4])
+    gather(4, 0)
+    took(4, 1)
+    gather(4, 1)
+    for q in range(3):
+        last_batch(q)
 
     @pl.loop(0, NF)
     def _(p):
@@ -294,27 +342,7 @@
             total = total + jnp.where(ids[0, t] == r, prod[t], 0.0)
         acc[:, pl.ds(pl.multiple_of(p * 128, 128), 128)] = total
 
-    took(3, 0)
-    pass_on(3, 4, 0, up)
-    took(5, 0)
-    arrived(idx_in.at[6], irecv.at[6])
-    gather(6)
-    took(3, 1)
-    took(5, 1)
-    pass_on(5, 4, 1, down)
-    arrived(idx_in.at[3], irecv.at[3])
-    gather(3)
-    merge_and_send(2)
-    arrived(idx_in.at[5], irecv.at[5])
-    gather(5)
     scatter(0)
-    took(4, 0)
-    took(4, 1)
-    arrived(idx_in.at[4], irecv.at[4])
-    gather(4)
-    for q in range(3):
-        last_batch(q)
-
     scatter(1)
     scatter(2)
     loads[6].wait()
@@ -323,7 +351,7 @@
     pre[...] = dot(frows[...].reshape(768, 128).T, s1[...])
     for q in range(3):
         for k in range(1, NX):
-            arrived(in1.at[3, mod(xc + NX - k, NX), pl.ds(0, COLS), pl.ds(q * 128, 128)], xrecv.at[3 + q, k])
+            arrived(in1.at[3, mod(xc + NX - k, NX), pl.ds(0, COLS), pl.ds(q * 128, 128)], xrecv.at[6 + q, k])
         scatter_part(3, q)
         for i in range(4):
             place = mod(lax.div(f, 3) + i, 4)
@@ -419,26 +447,41 @@
         caught(1, k)
     caught(0, 6)
 
-    for j in range(4):
-        got = dot_nt(oh2[j * 256 : j * 256 + 256], z[...])
-        out2[j * 256 : j * 256 + 256] = got[:, 0:128].astype(BF)
+    def quarter(j):
+        base = mod(lax.div(d, 16) + j, 4) * 16
+        rows = pl.ds(pl.multiple_of(base * 16, 256), 256)
+        got = dot_nt(oh2[rows], z[...])
+        out2[rows] = got[:, 0:128].astype(BF)
         rest = got[:, 128:160]
         for half in range(2):
-            outb[j * 2 + half] = jnp.concatenate(
+            outb[lax.div(base, 8) + half] = jnp.concatenate(
                 [rest[(half * 8 + i) * 16 : (half * 8 + i) * 16 + 16] for i in range(NX)], axis=1
             ).astype(BF)
+
+    def straight(j):
+        base = mod(lax.div(d, 16) + j, 4) * 16
+
+        @pl.loop(0, 16)
+        def _(k):
+            to = base + mod(d + k, 16)
+
+            @pl.when(to != d)
+            def _():
+                remote(
+                    out2.at[pl.ds(pl.multiple_of(to * 16, 16), 16)], in2.at[pl.ds(pl.multiple_of(d * 16, 16), 16)],
+                    asend, arecv, f, to,
+                ).start()
+
+    quarter(2)
+    straight(2)
+    for j in (0, 1, 3):
+        quarter(j)
     for k in range(1, NY):
         to = mod(y + k, NY)
         go(remote(outb.at[to], inb.at[y], bsend.at[0, k], brecv.at[0, k], f, to * NX + xc))
     inb[y] = outb[y]
-
-    @pl.loop(1, ND)
-    def _(k):
-        to = mod(d + k, ND)
-        remote(
-            out2.at[pl.ds(pl.multiple_of(to * 16, 16), 16)], in2.at[pl.ds(pl.multiple_of(d * 16, 16), 16)],
-            asend, arecv, f, to,
-        ).start()
+    for j in (1, 3, 0):
+        straight(j)
 
     mine = pl.ds(pl.multiple_of(d * 16, 16), 16)
     in2[mine] = out2[mine]
@@ -502,8 +545,8 @@
             pltpu.VMEM((768, HID), BF),
             pltpu.VMEM((768, HID), BF),
             pltpu.VMEM((NY, COLS, NODES), BF),
-            pltpu.VMEM((NY, 16, 128), I32),
-            pltpu.VMEM((NY, 16, 128), I32),
+            pltpu.VMEM((NY, 16, 128), I16),
+            pltpu.VMEM((NY, 16, 128), I16),
             pltpu.VMEM((NY, COLS, NODES), BF),
             pltpu.VMEM((4, NX, COLS, 384), BF),
             pltpu.VMEM((4, NX, 80, 384), BF),
@@ -534,7 +577,7 @@
             dma((NY, 2)), dma((NY, 2)),
             dma((NY,)), dma((NY,)),
             dma((NF,)), dma((NF,)),
-            dma((6, NX)), dma((6, NX)),
+            dma((9, NX)), dma((9, NX)),
             dma((NF,)), dma((NF,)),
             dma((2, 7)), dma((2, 7)),
             dma, dma,

time: 87.4 us -> 85.5 us (0.978)
  Pallas kernels: 86.6 us -> 84.7 us
    pallas_call x1, Pallas kernels: 84.9 us -> 83 us  [on_device(): pl.pallas_call(kernel, out_shape=(jax.ShapeDtypeStruct((128, HID), BF), j...]
where the time goes in v4:
time: 85.5 us; the launch traced here: 85.4 us
  Pallas kernels  84.7 us (99%)
    pallas_call x1, Pallas kernels, on_device(): pl.pallas_call(kernel, out_shape=(jax.ShapeDtypeStruct((128, HID), BF), j...  83 us

profile of v4, /device:TPU:1, one launch (start us, length us, event | category | flops | bytes accessed | tf_op | source)
XLA Modules:
  0.0 85.4 jit_solution(16034461948760352459)
XLA Ops:
  0.6 83.0 %shard_map.122 = (bf16[128,1024]{1,0:T(8,128)(2,1)}, f32[153,1,128]{2,1,0:T(1,128)}) custom-call(s32[2,36]{1,0:T(2,128)} %bitcast.29, s32[12,1,64]{2,1,0:T(1,128)} %bitcast.28, s32[12,16,64]{2,1,0:T(8,128)} %bitcast.25, s32[12,16,64]{2,1,0:T(8,128)} %bitcast.26, bf16[12,16,64]{2,1,0:T(8,128)(2,1)} %bitcast.27, bf16[64,1536]{1,0:T(8,128)(2,1)} %bitcast.24, ...), custom_call_target="tpu_custom_call" | custom-call | tf_op jit(solution)/shard_map/pallas_call | solution.py:531
  83.7 1.7 %shard_map.123 = (bf16[128,1024]{1,0:T(8,128)(2,1)}, f32[153,1,128]{2,1,0:T(1,128)}) custom-call(bf16[128,1024]{1,0:T(8,128)(2,1)} %get-tuple-element.6.hidden_ref, f32[153,1,128]{2,1,0:T(1,128)} %get-tuple-element.7.logits_ref), custom_call_target="tpu_custom_call" | custom-call | tf_op jit(solution)/shard_map/pallas_call | solution.py:602

commit v5 on v4

--- a/solution.py
+++ b/solution.py
@@ -85,6 +85,35 @@
     for load in loads:
         load.start()
 
+    pl.semaphore_wait(barrier, NY - 1 + NX - 1 + NF - 1)
+
+    sent = []
+
+    def go(copy):
+        copy.start()
+        sent.append(copy)
+
+    def table(slot):
+        return feat if slot == 0 else tab.at[slot]
+
+    def travels(slot):
+        return feat_hbm if slot == 0 else tab.at[slot]
+
+    def pass_on(from_slot, to_slot, half, di):
+        part = pl.ds(half * 32, 32)
+        go(remote(
+            travels(from_slot).at[part], tab.at[to_slot, part],
+            tsend.at[to_slot, half], trecv.at[to_slot, half], f, di,
+        ))
+
+    def took(slot, half):
+        arrived(tab.at[slot, pl.ds(half * 32, 32)], trecv.at[slot, half])
+
+    up = row_peer(1)
+    down = row_peer(NY - 1)
+    for half in range(2):
+        pass_on(0, 1, half, up)
+        pass_on(0, 7, half, down)
     spread_out = [place * 3 + third for third in range(3) for place in range(4)]
 
     loads[0].wait()
@@ -107,41 +136,15 @@
         idx_out[row] = jnp.concatenate(some, axis=0).astype(I16)
     idx_in[0] = idx_out[y]
 
-    loads[1].wait()
-    pl.semaphore_wait(barrier, NY - 1 + NX - 1 + NF - 1)
-
-    sent = []
-
-    def go(copy):
-        copy.start()
-        sent.append(copy)
-
-    def table(slot):
-        return feat if slot == 0 else tab.at[slot]
-
-    def pass_on(from_slot, to_slot, half, di):
-        part = pl.ds(half * 32, 32)
-        go(remote(
-            table(from_slot).at[part], tab.at[to_slot, part],
-            tsend.at[to_slot, half], trecv.at[to_slot, half], f, di,
-        ))
-
-    def took(slot, half):
-        arrived(tab.at[slot, pl.ds(half * 32, 32)], trecv.at[slot, half])
-
-    up = row_peer(1)
-    down = row_peer(NY - 1)
-    for half in range(2):
-        pass_on(0, 1, half, up)
-        pass_on(0, 7, half, down)
     for k in range(1, NY):
         to = mod(y + k, NY)
         go(remote(idx_out.at[to], idx_in.at[k], isend.at[k], irecv.at[k], f, to * NX + xc))
     for k in range(1, NF):
         g = mod(f + k, NF)
         go(remote(
-            feat.at[:, pl.ds(pl.multiple_of(g * 128, 128), 128)], frows.at[f], fsend.at[k], frecv.at[k], g, d
+            feat_hbm.at[:, pl.ds(pl.multiple_of(g * 128, 128), 128)], frows.at[f], fsend.at[k], frecv.at[k], g, d
         ))
+    loads[1].wait()
     frows[f] = feat[:, pl.ds(pl.multiple_of(f * 128, 128), 128)]
 
     def gather(slot, half):
@@ -472,20 +475,14 @@
                     asend, arecv, f, to,
                 ).start()
 
-    quarter(2)
-    straight(2)
-    for j in (0, 1, 3):
+    for j in range(4):
         quarter(j)
     for k in range(1, NY):
         to = mod(y + k, NY)
         go(remote(outb.at[to], inb.at[y], bsend.at[0, k], brecv.at[0, k], f, to * NX + xc))
     inb[y] = outb[y]
-    for j in (1, 3, 0):
-        straight(j)
-
-    mine = pl.ds(pl.multiple_of(d * 16, 16), 16)
-    in2[mine] = out2[mine]
-    total = dot_nt(band[...], z[...])
+    straight(2)
+    straight(1)
 
     for k in range(1, NY):
         arrived(inb.at[mod(y + NY - k, NY)], brecv.at[0, k])
@@ -497,6 +494,13 @@
         to = mod(xc + k, NX)
         go(remote(outb2.at[to], inb2.at[xc], bsend.at[1, k], brecv.at[1, k], f, y * NX + to))
     inb2[xc] = outb2[xc]
+    straight(3)
+    straight(0)
+    mine = pl.ds(pl.multiple_of(d * 16, 16), 16)
+    in2[mine] = out2[mine]
+    total = dot_nt(band[...], z[...])
+
+
     for k in range(1, NX):
         arrived(inb2.at[mod(xc + NX - k, NX)], brecv.at[1, k])
     flat = inb2[...].reshape(128, 256).astype(F32)

time: 85.5 us -> 87.5 us (1.023)
  Pallas kernels: 84.7 us -> 86.7 us
    pallas_call x1, Pallas kernels: 83 us -> 85 us  [on_device(): pl.pallas_call(kernel, out_shape=(jax.ShapeDtypeStruct((128, HID), BF), j...]
where the time goes in v5:
time: 87.5 us; the launch traced here: 87.3 us
  Pallas kernels  86.7 us (99%)
    pallas_call x1, Pallas kernels, on_device(): pl.pallas_call(kernel, out_shape=(jax.ShapeDtypeStruct((128, HID), BF), j...  85 us

profile of v5, /device:TPU:1, one launch (start us, length us, event | category | flops | bytes accessed | tf_op | source)
XLA Modules:
  0.0 87.3 jit_solution(11222290925674216353)
XLA Ops:
  0.6 85.0 %shard_map.122 = (bf16[128,1024]{1,0:T(8,128)(2,1)}, f32[153,1,128]{2,1,0:T(1,128)}) custom-call(s32[2,36]{1,0:T(2,128)} %bitcast.29, s32[12,1,64]{2,1,0:T(1,128)} %bitcast.28, s32[12,16,64]{2,1,0:T(8,128)} %bitcast.25, s32[12,16,64]{2,1,0:T(8,128)} %bitcast.26, bf16[12,16,64]{2,1,0:T(8,128)(2,1)} %bitcast.27, bf16[64,1536]{1,0:T(8,128)(2,1)} %bitcast.24, ...), custom_call_target="tpu_custom_call" | custom-call | tf_op jit(solution)/shard_map/pallas_call | solution.py:535
  85.6 1.7 %shard_map.123 = (bf16[128,1024]{1,0:T(8,128)(2,1)}, f32[153,1,128]{2,1,0:T(1,128)}) custom-call(bf16[128,1024]{1,0:T(8,128)(2,1)} %get-tuple-element.6.hidden_ref, f32[153,1,128]{2,1,0:T(1,128)} %get-tuple-element.7.logits_ref), custom_call_target="tpu_custom_call" | custom-call | tf_op jit(solution)/shard_map/pallas_call | solution.py:606

commit v6 on v5

--- a/solution.py
+++ b/solution.py
@@ -135,6 +135,7 @@
         some = [third[row * 4 : row * 4 + 4] for third in thirds] + [jnp.zeros((4, 128), I32)]
         idx_out[row] = jnp.concatenate(some, axis=0).astype(I16)
     idx_in[0] = idx_out[y]
+
 
     for k in range(1, NY):
         to = mod(y + k, NY)
@@ -475,14 +476,20 @@
                     asend, arecv, f, to,
                 ).start()
 
-    for j in range(4):
+    quarter(2)
+    straight(2)
+    for j in (0, 1, 3):
         quarter(j)
     for k in range(1, NY):
         to = mod(y + k, NY)
         go(remote(outb.at[to], inb.at[y], bsend.at[0, k], brecv.at[0, k], f, to * NX + xc))
     inb[y] = outb[y]
-    straight(2)
-    straight(1)
+    for j in (1, 3, 0):
+        straight(j)
+
+    mine = pl.ds(pl.multiple_of(d * 16, 16), 16)
+    in2[mine] = out2[mine]
+    total = dot_nt(band[...], z[...])
 
     for k in range(1, NY):
         arrived(inb.at[mod(y + NY - k, NY)], brecv.at[0, k])
@@ -494,13 +501,6 @@
         to = mod(xc + k, NX)
         go(remote(outb2.at[to], inb2.at[xc], bsend.at[1, k], brecv.at[1, k], f, y * NX + to))
     inb2[xc] = outb2[xc]
-    straight(3)
-    straight(0)
-    mine = pl.ds(pl.multiple_of(d * 16, 16), 16)
-    in2[mine] = out2[mine]
-    total = dot_nt(band[...], z[...])
-
-
     for k in range(1, NX):
         arrived(inb2.at[mod(xc + NX - k, NX)], brecv.at[1, k])
     flat = inb2[...].reshape(128, 256).astype(F32)

time: 87.5 us -> 85.3 us (0.975)
  Pallas kernels: 86.7 us -> 84.5 us
    pallas_call x1, Pallas kernels: 85 us -> 82.8 us  [on_device(): pl.pallas_call(kernel, out_shape=(jax.ShapeDtypeStruct((128, HID), BF), j...]
where the time goes in v6:
time: 85.3 us; the launch traced here: 85.2 us
  Pallas kernels  84.5 us (99%)
    pallas_call x1, Pallas kernels, on_device(): pl.pallas_call(kernel, out_shape=(jax.ShapeDtypeStruct((128, HID), BF), j...  82.8 us

profile of v6, /device:TPU:1, one launch (start us, length us, event | category | flops | bytes accessed | tf_op | source)
XLA Modules:
  0.0 85.2 jit_solution(7573133278932657094)
XLA Ops:
  0.6 82.8 %shard_map.122 = (bf16[128,1024]{1,0:T(8,128)(2,1)}, f32[153,1,128]{2,1,0:T(1,128)}) custom-call(s32[2,36]{1,0:T(2,128)} %bitcast.29, s32[12,1,64]{2,1,0:T(1,128)} %bitcast.28, s32[12,16,64]{2,1,0:T(8,128)} %bitcast.25, s32[12,16,64]{2,1,0:T(8,128)} %bitcast.26, bf16[12,16,64]{2,1,0:T(8,128)(2,1)} %bitcast.27, bf16[64,1536]{1,0:T(8,128)(2,1)} %bitcast.24, ...), custom_call_target="tpu_custom_call" | custom-call | tf_op jit(solution)/shard_map/pallas_call | solution.py:535
  83.4 1.7 %shard_map.123 = (bf16[128,1024]{1,0:T(8,128)(2,1)}, f32[153,1,128]{2,1,0:T(1,128)}) custom-call(bf16[128,1024]{1,0:T(8,128)(2,1)} %get-tuple-element.6.hidden_ref, f32[153,1,128]{2,1,0:T(1,128)} %get-tuple-element.7.logits_ref), custom_call_target="tpu_custom_call" | custom-call | tf_op jit(solution)/shard_map/pallas_call | solution.py:606
